TPU v7x, 256 devices: a whole 4x4x8 slice. The times are simulated.
256 devices in a mesh: dp: 32 (over y, z_lo, core), tensor: 8 (over z_hi, x).
Axes of the slice: x: 4, y: 4, z: 8 (z_hi: 2, z_lo: 4; z = z_hi * 4 + z_lo), core: 2. Of those that a mesh axis runs over, the one named last changes fastest.
Arguments:
- tokens: bfloat16 [8192, 4096], P('dp'), may hold values from -6 to 6
- gate_values: bfloat16 [8192, 14336], P('dp', 'tensor'), may hold values from -6 to 6
- up_latent: float32 [4096, 14336], P('dp', 'tensor'), may hold values from -6.25 to 6.25
- hidden_grad: bfloat16 [8192, 14336], P('dp', 'tensor'), may hold values from -100 to 100
Outputs:
- hidden: bfloat16 [8192, 14336], P('dp', 'tensor')
- gate_grad: bfloat16 [8192, 14336], P('dp', 'tensor')
- token_grad: bfloat16 [8192, 4096], P('dp', 'tensor')
- up_grad: float32 [4096, 14336], P('dp', 'tensor')
All inputs are finite; a program needn't handle non-finite values.
Results may differ from a plain program's by a relative error of at most 0.03.
Values may be sent and summed in bfloat16 or wider, within the bound.
A program may use at most 128 MiB of HBM per device.

v0:
```python
import jax
import jax.numpy as jnp
from jax import lax
from jax.sharding import PartitionSpec as P

D = 4096
FF = 14336


EPSILON = 1e-05


def ternarize(latent_half, scale_value):
    latent_wide = latent_half.astype(jnp.float32)
    keep = jnp.abs(latent_wide) > 0.5 * scale_value
    signs = jnp.where(keep, jnp.sign(latent_wide), jnp.float32(0.0))
    return (signs * scale_value).astype(jnp.bfloat16)


def on_device(tokens, gate_values, up_latent, hidden_grad):
    latent_half = up_latent.astype(jnp.bfloat16)
    local_total = jnp.sum(jnp.abs(latent_half), dtype=jnp.float32)
    whole_total = lax.psum(local_total, ("dp", "tensor"))
    scale_value = whole_total / (D * FF) + EPSILON
    ternary = ternarize(latent_half, scale_value)
    weight = lax.all_gather(ternary, "dp", axis=0, tiled=True)
    up_value = jnp.dot(tokens, weight, preferred_element_type=jnp.float32)
    gate_wide = gate_values.astype(jnp.float32)
    sigmoid_gate = jax.nn.sigmoid(gate_wide)
    activated = gate_wide * sigmoid_gate
    hidden = (activated * up_value).astype(jnp.bfloat16)
    cotangent = hidden_grad.astype(jnp.float32)
    up_cot = (cotangent * activated).astype(jnp.bfloat16)
    gate_grad = (
        cotangent * up_value * sigmoid_gate * (1.0 + gate_wide * (1.0 - sigmoid_gate))
    ).astype(jnp.bfloat16)
    token_term = lax.dot_general(
        up_cot, weight, (((1,), (1,)), ((), ())), preferred_element_type=jnp.float32
    )
    token_grad = lax.psum_scatter(
        token_term.astype(jnp.bfloat16), "tensor", scatter_dimension=1, tiled=True
    )
    up_grad = lax.psum_scatter(
        lax.dot_general(
            tokens, up_cot, (((0,), (0,)), ((), ())), preferred_element_type=jnp.float32
        ).astype(jnp.bfloat16),
        "dp",
        scatter_dimension=0,
        tiled=True,
    ).astype(jnp.float32)
    return (hidden, gate_grad, token_grad, up_grad)


def solution(mesh):
    placed = (P("dp", None), P("dp", "tensor"), P("dp", "tensor"), P("dp", "tensor"))
    return jax.shard_map(
        on_device,
        mesh=mesh,
        in_specs=placed,
        out_specs=(P("dp", "tensor"), P("dp", "tensor"), P("dp", "tensor"), P("dp", "tensor")),
        check_vma=False,
    )
```

profile of v0, /device:TPU:8, one launch (start us, length us, event | category | flops | bytes accessed | tf_op | source)
XLA Modules:
  0.0 465.7 jit_solution(14123245885748500420)
XLA Ops:
  7.2 0.0 copy-start
  7.2 0.0 all-gather.2.cloned.1.call-start
  7.2 2.2 convert_reduce_fusion
  9.4 78.5 %psum.7 = f32[]{:T(128)} all-reduce(f32[]{:T(128)} %convert_reduce_fusion), channel_id=1, replica_groups=mesh['dp'=32,'tensor'=8] {'dp','tensor'}, use_global_device_ids=true, to_apply=%region_1.0 | all-reduce | flops 1 | bytes 8 | tf_op jit(solution)/shard_map/psum | solution.py:23
  88.6 2.3 fusion.12
  90.9 0.0 all-gather.2.cloned.1.call-update
  90.9 0.0 reduce-scatter.7.cloned.1.call-start
  91.0 0.0 copy-done.1
  91.0 1.3 copy.13
  92.3 2.3 copy.14
  94.6 8.9 %fusion = bf16[4096,1792]{0,1:T(8,128)(2,1)} fusion(bf16[256,4096]{1,0:T(8,128)(2,1)S(1)} %copy-done, bf16[256,1792]{0,1:T(8,128)(2,1)} %copy.14, bf16[256,1792]{0,1:T(8,128)(2,1)S(1)} %copy-done.2), kind=kOutput, calls=%fused_computation.1 | convolution fusion | flops 3769106432 | bytes 18612224 | tf_op jit(solution)/shard_map/dot_general | solution.py:44
  103.5 18.9 %copy.18 = bf16[4096,1792]{1,0:T(8,128)(2,1)} copy(bf16[4096,1792]{0,1:T(8,128)(2,1)} %fusion) | data formatting | bytes 29360128
  122.4 0.0 reduce-scatter.7.cloned.1.call-update
  122.4 0.2 reduce-scatter.5.cloned.1.call-start
  122.6 54.7 %all-gather.2.cloned.1.call-done = bf16[4096,1792]{1,0:T(8,128)(2,1)} async-done(((bf16[128,1792]{1,0:T(8,128)(2,1)}), bf16[4096,1792]{1,0:T(8,128)(2,1)}) %all-gather.2.cloned.1.call-update) | async-done | bytes 14680080 | tf_op jit(solution)/shard_map/all_gather | solution.py:26
  177.3 11.0 %convolution_convert_fusion.1 = bf16[256,4096]{1,0:T(8,128)(2,1)} fusion(bf16[4096,1792]{1,0:T(8,128)(2,1)} %all-gather.2.cloned.1.call-done, bf16[256,1792]{0,1:T(8,128)(2,1)} %copy.14, bf16[256,1792]{0,1:T(8,128)(2,1)S(1)} %copy-done.2), kind=kOutput, calls=%fused_computation.2 | convolution fusion | flops 3762814976 | bytes 18612224 | tf_op jit(solution)/shard_map/dot_general | solution.py:37
  188.3 0.0 reduce-scatter.5.cloned.1.call-update
  188.3 11.7 %fusion.3 = (bf16[256,1792]{0,1:T(8,128)(2,1)}, bf16[256,1792]{0,1:T(8,128)(2,1)}) fusion(bf16[256,1792]{0,1:T(8,128)(2,1)} %copy.14, bf16[256,1792]{0,1:T(8,128)(2,1)S(1)} %copy-done.2, bf16[4096,1792]{1,0:T(8,128)(2,1)} %all-gather.2.cloned.1.call-done, bf16[256,4096]{1,0:T(8,128)(2,1)S(1)} %copy-done), kind=kOutput, calls=%fused_computation.11 | convolution fusion | flops 3764977664 | bytes 20447232 | tf_op jit(solution)/shard_map/dot_general | solution.py:27
  200.0 2.3 copy.16
  202.3 1.4 copy.15
  203.7 145.8 %reduce-scatter.7.cloned.1.call-done = bf16[128,1792]{1,0:T(8,128)(2,1)} async-done(((bf16[4096,1792]{1,0:T(8,128)(2,1)}), bf16[128,1792]{1,0:T(8,128)(2,1)}) %reduce-scatter.7.cloned.1.call-update) | async-done | bytes 458768
  349.5 1.3 copy.19
  350.7 1.1 copy.17
  351.9 107.3 %reduce-scatter.5.cloned.1.call-done = bf16[256,512]{1,0:T(8,128)(2,1)} async-done(((bf16[256,4096]{1,0:T(8,128)(2,1)}), bf16[256,512]{1,0:T(8,128)(2,1)}) %reduce-scatter.5.cloned.1.call-update) | async-done | bytes 262160 | tf_op jit(solution)/shard_map/reduce_scatter | solution.py:40
  (6 shorter events, 0.0 us)
Async XLA Ops:
  7.2 87.4 %copy-start = (bf16[256,4096]{1,0:T(8,128)(2,1)S(1)}, bf16[256,4096]{1,0:T(8,128)(2,1)}, u32[]{:S(2)}) copy-start(bf16[256,4096]{1,0:T(8,128)(2,1)} %param.4) | copy-start | bytes 6291460
  7.2 83.8 %copy-start.1 = (bf16[256,1792]{1,0:T(8,128)(2,1)S(1)}, bf16[256,1792]{1,0:T(8,128)(2,1)}, u32[]{:S(2)}) copy-start(bf16[256,1792]{1,0:T(8,128)(2,1)} %param.5) | copy-start | bytes 2752516
  7.2 170.1 %all-gather.2.cloned.1.call-start = ((), (), s32[]{:S(2)}) async-start(), calls=%async_computation.2 | async-start | bytes 15138816 | tf_op jit(solution)/shard_map/all_gather | solution.py:26
  90.9 258.5 %reduce-scatter.7.cloned.1.call-start = ((), (), s32[]{:S(2)}) async-start(), calls=%async_computation.4 | async-start | bytes 15138816
  92.3 2.3 copy-start.2
  122.4 336.8 %reduce-scatter.5.cloned.1.call-start = ((), (), s32[]{:S(2)}) async-start(), calls=%async_computation.3 | async-start | bytes 2359296 | tf_op jit(solution)/shard_map/reduce_scatter | solution.py:40
  200.0 2.3 copy-start.3
Sparse Core Ops, SparseCore 0:
  91.1 86.1 all-gather.1
  179.9 169.5 reduce-scatter.6
  354.1 105.0 reduce-scatter.4
where the time goes:
time: 467 us; the launch traced here: 466 us
  waiting for transfers between devices  308 us (66%)
  blocking collectives  78.5 us (17%)
  matrix products  31.6 us (7%)
  local copies, waits for them, and re-layouts  28.6 us (6%)
  between operations  14.4 us (3%)
    unnamed x4, waiting for transfers between devices  146 us
    reduce_scatter x1, waiting for transfers between devices, on_device(): lax.psum_scatter(token_term.astype(jnp.bfloat16), 'tensor', scatter_dimen...  107 us
    psum x1, blocking collectives, on_device(): whole_total = lax.psum(local_total, ('dp', 'tensor'))  78.5 us
    all_gather x1, waiting for transfers between devices, on_device(): weight = lax.all_gather(ternary, 'dp', axis=0, tiled=True)  54.7 us
    unnamed x15, local copies, waits for them, and re-layouts  28.6 us
    dot_general x1, matrix products, on_device(): up_value = jnp.dot(tokens, weight, preferred_element_type=jnp.float32)  11.7 us
    dot_general x1, matrix products, on_device(): lax.dot_general(up_cot, weight, (((1,), (1,)), ((), ())), preferred_eleme...  11 us
  transfers between devices with their start and end apart: 3, of which 3 were waited for; matrix products, arithmetic and copies ran while one was open for 13% of the time, Pallas kernels for 0%

commit v1 on v0

v1 whole, which is shorter than its diff:
```python
import functools

import jax
import jax.numpy as jnp
from jax import lax
from jax.experimental import pallas as pl
from jax.experimental.pallas import tpu as pltpu
from jax.sharding import PartitionSpec as P

D = 4096
FF = 14336
TOK = 256
COLS = 1792
HALF = COLS // 2
ROWS = 128
BLOCK = 1024
EPSILON = 1e-05
MESH = pl.DeviceIdType.MESH
F32 = jnp.float32
BF16 = jnp.bfloat16


def kernel(
    tokens, gate, latent, cot,
    hidden_out, gate_out, token_out, up_out,
    lat32, wg, wt, tokg, tokt, ucg, gate_v, cot_v,
    gp, gxs, gxr, gsend, grl, grr,
    pvf, pvs, fwd, chain, direct,
    tt_own, tt_send, tt_recv, zsend, zrecv, fsend, tgr,
    s1, s2, s3,
    in_sem, zr_sem, zsr_sem, zsl_sem, cs_sem, cr_sem,
    yrs, yrr, yls, ylr, tks, tkr,
    s1s, s1r, s2s, s2r, s3s, s3r,
    gcs, gcr, gls, glr, grs, grr_sem,
    ops, opr, tts, ttr, zxs, zxr, fs, fr,
):
    me_dp = lax.axis_index("dp")
    me_t = lax.axis_index("tensor")
    y = me_dp // 8
    g8 = me_dp % 8
    zl = g8 // 2
    k = g8 % 2
    x = me_t % 4
    zh = me_t // 4

    def dp_of(yy, zz, kk):
        return yy * 8 + zz * 2 + kk

    def at_y(d):
        return (((y + d) % 4) * 8 + g8, me_t)

    def at_z(zz):
        return (dp_of(y, zz, k), me_t)

    other = (dp_of(y, zl, 1 - k), me_t)

    def at_x(d):
        return (me_dp, zh * 4 + (x + d) % 4)

    flip = (me_dp, (1 - zh) * 4 + x)

    def rcopy(src, dst, ssem, rsem, dev):
        return pltpu.make_async_remote_copy(
            src_ref=src, dst_ref=dst, send_sem=ssem, recv_sem=rsem,
            device_id=dev, device_id_type=MESH,
        )

    source_x, source_y = y, 2 * zh + x // 2
    self_source = jnp.logical_and(source_x == x, source_y == y)
    collects = zh == y // 2

    def final_dev(j):
        return (dp_of(x, zl, k), zh * 4 + 2 * (y % 2) + j)

    def final_self(j):
        return jnp.logical_and(x == y, 2 * (y % 2) + j == x)

    lat_in = pltpu.make_async_copy(latent, lat32, in_sem.at[0])
    gate_in = pltpu.make_async_copy(gate, gate_v, in_sem.at[1])
    cot_in = pltpu.make_async_copy(cot, cot_v, in_sem.at[2])
    tok_in = pltpu.make_async_copy(
        tokens.at[:, pl.ds(pl.multiple_of(y * BLOCK, BLOCK), BLOCK)],
        tokg.at[pl.ds(pl.multiple_of(y * TOK, TOK), TOK)],
        in_sem.at[3],
    )
    lat_in.start()
    gate_in.start()
    cot_in.start()
    tok_in.start()

    barrier = pltpu.get_barrier_semaphore()

    def greet(dev):
        pl.semaphore_signal(barrier, inc=1, device_id=dev, device_id_type=MESH)

    for d in range(1, 4):
        greet(at_y(d))
    for d in range(1, 8):
        greet((y * 8 + (g8 + d) % 8, me_t))
        greet((me_dp, (me_t + d) % 8))

    @pl.when(jnp.logical_not(self_source))
    def _():
        greet((dp_of(source_y, zl, k), zh * 4 + source_x))

    takers = jnp.int32(2)
    for j in range(2):
        takers = takers - jnp.where(final_self(j), 1, 0)
    pl.semaphore_wait(barrier, 17 + jnp.where(collects, takers, 0))

    def tok_send(d):
        yy = (y + d) % 4
        return rcopy(
            tokens.at[:, pl.ds(pl.multiple_of(yy * BLOCK, BLOCK), BLOCK)],
            tokg.at[pl.ds(pl.multiple_of(y * TOK, TOK), TOK)],
            tks.at[d], tkr.at[d], at_y(d),
        )

    for d in (1, 3, 2):
        tok_send(d).start()

    lat_in.wait()
    part = jnp.zeros((8, 128), F32)

    def cast_rows(i, acc):
        rows = pl.ds(pl.multiple_of(i * 16, 16), 16)
        half = lat32[rows, :].astype(BF16)
        wg[zl, k, rows, :] = half
        mag = jnp.abs(half.astype(F32))
        mag = mag[0:8] + mag[8:16]
        tot = mag[:, 0:128]
        for c in range(1, COLS // 128):
            tot = tot + mag[:, c * 128:(c + 1) * 128]
        return acc + tot

    part = lax.fori_loop(0, ROWS // 16, cast_rows, part)

    def z_right(b):
        return rcopy(wg.at[b, k], wg.at[b, k], zsr_sem.at[b], zr_sem.at[b], at_z(lax.rem(zl + 1, 4)))

    def z_left(b):
        return rcopy(wg.at[b, k], wg.at[b, k], zsl_sem.at[b], zr_sem.at[b], at_z(lax.rem(zl + 3, 4)))

    def c_send(b):
        return rcopy(wg.at[b, k], wg.at[b, k], cs_sem.at[b], cr_sem.at[b], other)

    def c_recv(b):
        return rcopy(wg.at[b, k], wg.at[b, 1 - k], cs_sem.at[b], cr_sem.at[b], other)

    @pl.when(zl < 3)
    def _():
        z_right(zl).start()

    @pl.when(zl > 0)
    def _():
        z_left(zl).start()

    c_send(zl).start()

    s1[g8] = part

    def s1_copy(d):
        return rcopy(s1.at[g8], s1.at[g8], s1s.at[d], s1r.at[d], (y * 8 + (g8 + d) % 8, me_t))

    def s2_copy(d):
        return rcopy(s2.at[y], s2.at[y], s2s.at[d], s2r.at[d], at_y(d))

    def s3_copy(d):
        return rcopy(s3.at[me_t], s3.at[me_t], s3s.at[d], s3r.at[d], (me_dp, (me_t + d) % 8))

    for d in range(1, 8):
        s1_copy(d).start()

    gate_in.wait()
    cot_in.wait()

    def cot_rows(lo, hi):
        @pl.loop(lo // 16, hi // 16)
        def _(i):
            rows = pl.ds(pl.multiple_of(i * 16, 16), 16)
            g = gate_v[rows, :].astype(F32)
            act = g * jax.nn.sigmoid(g)
            to = pl.ds(pl.multiple_of(y * TOK + i * 16, 16), 16)
            ucg[to, :] = (cot_v[rows, :].astype(F32) * act).astype(BF16)

    def uc_half(yy, h):
        return ucg.at[pl.ds(pl.multiple_of((yy % 4) * TOK + h * 128, 128), 128)]

    def y_right(i):
        piece = (uc_half(y, 0), uc_half(y, 1), uc_half(y + 3, 0))[i]
        return rcopy(piece, piece, yrs.at[i], yrr.at[i], at_y(1))

    def y_left(i):
        piece = (uc_half(y, 1), uc_half(y, 0), uc_half(y + 1, 1))[i]
        return rcopy(piece, piece, yls.at[i], ylr.at[i], at_y(3))

    cot_rows(0, 128)
    y_right(0).start()
    cot_rows(128, 256)
    y_left(0).start()
    y_right(1).start()
    y_left(1).start()

    for d in range(1, 8):
        s1_copy(d).wait_recv()
    tot = s1[0]
    for i in range(1, 8):
        tot = tot + s1[i]
    s2[y] = tot
    for d in range(1, 4):
        s2_copy(d).start()
    for d in range(1, 4):
        s2_copy(d).wait_recv()
    tot = s2[0]
    for i in range(1, 4):
        tot = tot + s2[i]
    s3[me_t] = tot
    for d in range(1, 8):
        s3_copy(d).start()
    for d in range(1, 8):
        s3_copy(d).wait_recv()
    tot = s3[0]
    for i in range(1, 8):
        tot = tot + s3[i]
    total = jnp.sum(jnp.sum(tot, axis=0, keepdims=True), axis=1, keepdims=True)
    scale = total / (D * FF) + EPSILON

    def z_step(s):
        left, right = zl - s, zl + s

        @pl.when(left >= 0)
        def _():
            b = lax.rem(left + 4, 4)
            z_right(b).wait_recv()

            @pl.when(zl < 3)
            def _():
                z_right(b).start()

            c_send(b).start()

        @pl.when(right <= 3)
        def _():
            b = lax.rem(right, 4)
            z_left(b).wait_recv()

            @pl.when(zl > 0)
            def _():
                z_left(b).start()

            c_send(b).start()

    z_step(1)
    y_right(0).wait_recv()
    y_right(2).start()
    y_left(0).wait_recv()
    y_left(2).start()
    z_step(2)
    y_right(1).wait_recv()
    y_left(1).wait_recv()
    tok_in.wait()
    for d in (1, 3, 2):
        tok_send(d).wait_recv()
    z_step(3)
    for b in range(4):
        c_recv(b).wait_recv()

    bound = 0.5 * scale
    plus = scale.astype(BF16).astype(F32)

    @pl.loop(0, BLOCK // 16)
    def _(i):
        b, r = i // 16, i % 16
        wide = wg[b, r // 8, pl.ds(pl.multiple_of((r % 8) * 16, 16), 16), :].astype(F32)
        tern = jnp.where(wide > bound, plus, jnp.where(wide < -bound, -plus, 0.0))
        wt[pl.ds(pl.multiple_of(i * 16, 16), 16), :] = tern.astype(BF16)

    y_right(2).wait_recv()
    y_left(2).wait_recv()

    def m1(target):
        cols = pl.ds(pl.multiple_of(target * 256, 256), 256)
        tokt[...] = tokg[:, cols].T

        @pl.loop(0, 7)
        def _(n):
            at = pl.ds(pl.multiple_of(n * 256, 256), 256)
            gp[target, :, at] = jnp.dot(tokt[...], ucg[:, at], preferred_element_type=F32)

        theirs = pl.ds(pl.multiple_of((1 - k) * ROWS, ROWS), ROWS)
        gxs[target] = gp[target, theirs, :].astype(BF16)
        g_cross(target).start()

    def g_cross(target):
        return rcopy(gxs.at[target], gxr.at[target], gcs.at[target], gcr.at[target], other)

    def g_right(target):
        return rcopy(gsend.at[target], grl.at[target], grs.at[target], glr.at[target], at_z(lax.rem(zl + 1, 4)))

    def g_left(target):
        return rcopy(gsend.at[target], grr.at[target], gls.at[target], grr_sem.at[target], at_z(lax.rem(zl + 3, 4)))

    mine = pl.ds(pl.multiple_of(k * ROWS, ROWS), ROWS)

    def combine(target):
        g_cross(target).wait_recv()

        @pl.when(target > zl)
        def _():
            @pl.when(zl == 0)
            def _():
                gsend[target] = (gp[target, mine, :] + gxr[target].astype(F32)).astype(BF16)

            @pl.when(zl > 0)
            def _():
                g_right(target).wait_recv()
                gsend[target] = (
                    gp[target, mine, :] + gxr[target].astype(F32) + grl[target].astype(F32)
                ).astype(BF16)

            g_right(target).start()

        @pl.when(target < zl)
        def _():
            @pl.when(zl == 3)
            def _():
                gsend[target] = (gp[target, mine, :] + gxr[target].astype(F32)).astype(BF16)

            @pl.when(zl < 3)
            def _():
                g_left(target).wait_recv()
                gsend[target] = (
                    gp[target, mine, :] + gxr[target].astype(F32) + grr[target].astype(F32)
                ).astype(BF16)

            g_left(target).start()

    def pick(a0, a1, a2, a3):
        return jnp.where(zl == 0, a0, jnp.where(zl == 1, a1, jnp.where(zl == 2, a2, a3)))

    order = [pick(3, 3, 0, 0), pick(2, 0, 3, 1), pick(1, 2, 1, 2), zl]
    edge = jnp.logical_or(zl == 0, zl == 3)

    def m2(slot, yy):
        rows = pl.ds(pl.multiple_of((yy % 4) * TOK, TOK), TOK)

        @pl.loop(0, 7)
        def _(n):
            at = pl.ds(pl.multiple_of(n * 256, 256), 256)
            pvf[slot, :, at] = jnp.dot(tokg[rows, :], wt[:, at], preferred_element_type=F32)

    A, B = pl.ds(0, HALF), pl.ds(HALF, HALF)

    def p_minus(i):
        slot, cols = ((0, A), (1, B), (1, A))[i]
        dst = (fwd, direct, chain)[i]
        return rcopy(pvs.at[slot, :, cols], dst.at[:, cols], ops.at[0, i], opr.at[0, i], at_y(3))

    def p_plus(i):
        slot, cols = ((0, B), (2, A), (2, B))[i]
        dst = (fwd, direct, chain)[i]
        return rcopy(pvs.at[slot, :, cols], dst.at[:, cols], ops.at[1, i], opr.at[1, i], at_y(1))

    m1(order[0])
    m2(0, y + 2)
    pvs[0] = pvf[0].astype(BF16)
    p_minus(0).start()
    p_plus(0).start()

    @pl.when(edge)
    def _():
        combine(order[0])

    m2(1, y + 3)
    pvs[1, :, B] = pvf[1, :, B].astype(BF16)
    p_minus(1).start()
    m2(2, y + 1)
    pvs[2, :, A] = pvf[2, :, A].astype(BF16)
    p_plus(1).start()

    def m3(xx):
        rows = pl.ds(pl.multiple_of(xx * TOK, TOK), TOK)

        @pl.loop(0, 4)
        def _(n):
            at = pl.ds(pl.multiple_of(n * 256, 256), 256)
            tt_own[:, at] = lax.dot_general(
                ucg[rows, :], wt[at, :], (((1,), (1,)), ((), ())), preferred_element_type=F32
            )

    def t_send(d):
        return rcopy(tt_send.at[d - 1], tt_recv.at[d - 1], tts.at[d], ttr.at[d], at_x(d))

    for d in (2, 1, 3):
        m3((x + d) % 4)
        tt_send[d - 1] = tt_own[...].astype(BF16)
        t_send(d).start()
    m3(x)

    m1(order[1])

    @pl.when(edge)
    def _():
        combine(order[1])

    m1(order[2])

    @pl.when(edge)
    def _():
        combine(order[2])

    m1(order[3])

    @pl.when(jnp.logical_not(edge))
    def _():
        combine(order[0])

    p_minus(0).wait_recv()
    pvs[1, :, A] = (pvf[1, :, A] + fwd[:, A].astype(F32)).astype(BF16)
    p_minus(2).start()
    p_plus(0).wait_recv()
    pvs[2, :, B] = (pvf[2, :, B] + fwd[:, B].astype(F32)).astype(BF16)
    p_plus(2).start()

    m2(0, y)

    @pl.when(jnp.logical_not(edge))
    def _():
        combine(order[1])
        combine(order[2])

    for d in range(1, 4):
        t_send(d).wait_recv()

    @pl.loop(0, TOK // 16)
    def _(i):
        rows = pl.ds(pl.multiple_of(i * 16, 16), 16)
        total = tt_own[rows, :]
        for d in range(3):
            total = total + tt_recv[d, rows, :].astype(F32)
        tt_own[rows, :] = total
        zsend[rows, :] = total.astype(BF16)

    z_copy = rcopy(zsend, zrecv, zxs, zxr, flip)

    @pl.when(jnp.logical_not(collects))
    def _():
        z_copy.start()

    def f_send(j):
        return rcopy(fsend.at[j], tgr, fs.at[j], fr, final_dev(j))

    @pl.when(collects)
    def _():
        z_copy.wait_recv()
        for j in range(2):
            cols = pl.ds(j * 512, 512)
            fsend[j] = (tt_own[:, cols] + zrecv[:, cols].astype(F32)).astype(BF16)

            @pl.when(jnp.logical_not(final_self(j)))
            def _():
                f_send(j).start()

            @pl.when(final_self(j))
            def _():
                tgr[...] = fsend[j]

    p_minus(1).wait_recv()
    p_plus(1).wait_recv()
    p_minus(2).wait_recv()
    p_plus(2).wait_recv()

    @pl.loop(0, TOK // 16)
    def _(i):
        rows = pl.ds(pl.multiple_of(i * 16, 16), 16)
        up = pvf[0, rows, :] + chain[rows, :].astype(F32) + direct[rows, :].astype(F32)
        g = gate_v[rows, :].astype(F32)
        sig = jax.nn.sigmoid(g)
        hidden_out[rows, :] = (g * sig * up).astype(BF16)
        gate_out[rows, :] = (
            cot_v[rows, :].astype(F32) * up * sig * (1.0 + g * (1.0 - sig))
        ).astype(BF16)

    g_cross(zl).wait_recv()
    up_out[...] = gp[zl, mine, :] + gxr[zl].astype(F32)

    @pl.when(zl > 0)
    def _():
        g_right(zl).wait_recv()
        up_out[...] += grl[zl].astype(F32)

    @pl.when(zl < 3)
    def _():
        g_left(zl).wait_recv()
        up_out[...] += grr[zl].astype(F32)

    @pl.when(jnp.logical_not(self_source))
    def _():
        f_send(0).wait_recv()

    token_out[...] = tgr[...]

    for d in range(1, 4):
        tok_send(d).wait_send()
        s2_copy(d).wait_send()
        t_send(d).wait_send()
    for d in range(1, 8):
        s1_copy(d).wait_send()
        s3_copy(d).wait_send()
    for i in range(3):
        y_right(i).wait_send()
        y_left(i).wait_send()
        p_minus(i).wait_send()
        p_plus(i).wait_send()
    for b in range(4):
        c_send(b).wait_send()
        g_cross(b).wait_send()

        @pl.when(jnp.logical_and(zl < 3, b <= zl))
        def _():
            z_right(b).wait_send()

        @pl.when(jnp.logical_and(zl > 0, b >= zl))
        def _():
            z_left(b).wait_send()

        @pl.when(b > zl)
        def _():
            g_right(b).wait_send()

        @pl.when(b < zl)
        def _():
            g_left(b).wait_send()

    @pl.when(jnp.logical_not(collects))
    def _():
        z_copy.wait_send()

    for j in range(2):
        @pl.when(jnp.logical_and(collects, jnp.logical_not(final_self(j))))
        def _():
            f_send(j).wait_send()


def on_device(tokens, gate_values, up_latent, hidden_grad):
    dma = pltpu.SemaphoreType.DMA
    vm = pltpu.VMEM
    return pl.pallas_call(
        kernel,
        out_shape=(
            jax.ShapeDtypeStruct((TOK, COLS), BF16),
            jax.ShapeDtypeStruct((TOK, COLS), BF16),
            jax.ShapeDtypeStruct((TOK, 512), BF16),
            jax.ShapeDtypeStruct((ROWS, COLS), F32),
        ),
        in_specs=[pl.BlockSpec(memory_space=pl.ANY)] * 4,
        out_specs=(pl.BlockSpec(memory_space=pltpu.VMEM),) * 4,
        scratch_shapes=[
            vm((ROWS, COLS), F32),
            vm((4, 2, ROWS, COLS), BF16),
            vm((BLOCK, COLS), BF16),
            vm((BLOCK, BLOCK), BF16),
            vm((256, BLOCK), BF16),
            vm((BLOCK, COLS), BF16),
            vm((TOK, COLS), BF16),
            vm((TOK, COLS), BF16),
            vm((4, 256, COLS), F32),
            vm((4, ROWS, COLS), BF16),
            vm((4, ROWS, COLS), BF16),
            vm((4, ROWS, COLS), BF16),
            vm((4, ROWS, COLS), BF16),
            vm((4, ROWS, COLS), BF16),
            vm((3, TOK, COLS), F32),
            vm((3, TOK, COLS), BF16),
            vm((TOK, COLS), BF16),
            vm((TOK, COLS), BF16),
            vm((TOK, COLS), BF16),
            vm((TOK, BLOCK), F32),
            vm((3, TOK, BLOCK), BF16),
            vm((3, TOK, BLOCK), BF16),
            vm((TOK, BLOCK), BF16),
            vm((TOK, BLOCK), BF16),
            vm((2, TOK, 512), BF16),
            vm((TOK, 512), BF16),
            vm((8, 8, 128), F32),
            vm((4, 8, 128), F32),
            vm((8, 8, 128), F32),
            dma((4,)),
            dma((4,)), dma((4,)), dma((4,)), dma((4,)), dma((4,)),
            dma((3,)), dma((3,)), dma((3,)), dma((3,)), dma((4,)), dma((4,)),
            dma((8,)), dma((8,)), dma((4,)), dma((4,)), dma((8,)), dma((8,)),
            dma((4,)), dma((4,)), dma((4,)), dma((4,)), dma((4,)), dma((4,)),
            dma((2, 3)), dma((2, 3)), dma((4,)), dma((4,)), dma, dma, dma((2,)), dma,
        ],
        compiler_params=pltpu.CompilerParams(
            collective_id=0, has_side_effects=True, vmem_limit_bytes=60 * 1024 * 1024
        ),
    )(tokens, gate_values, up_latent, hidden_grad)


def solution(mesh):
    placed = (P("dp", None), P("dp", "tensor"), P("dp", "tensor"), P("dp", "tensor"))
    return jax.shard_map(
        on_device,
        mesh=mesh,
        in_specs=placed,
        out_specs=(P("dp", "tensor"), P("dp", "tensor"), P("dp", "tensor"), P("dp", "tensor")),
        check_vma=False,
    )
```

time: 467 us -> 170 us (0.36)
  the two profiles are of different devices: /device:TPU:8 before, /device:TPU:56 now
where the time goes in v1:
time: 170 us
  Pallas kernels  164 us (96%)
  local copies, waits for them, and re-layouts  4.87 us (3%)
    pallas_call x1, Pallas kernels, on_device(): pl.pallas_call(kernel, out_shape=(jax.ShapeDtypeStruct((TOK, COLS), BF16)...  164 us
    unnamed x10, local copies, waits for them, and re-layouts  4.87 us

profile of v1, /device:TPU:56, one launch (start us, length us, event | category | flops | bytes accessed | tf_op | source)
XLA Modules:
  0.0 170.0 jit_solution(8563811103186386310)
XLA Ops:
  0.6 164.4 %shard_map.75 = (bf16[256,1792]{1,0:T(8,128)(2,1)}, bf16[256,1792]{1,0:T(8,128)(2,1)}, bf16[256,512]{1,0:T(8,128)(2,1)}, f32[128,1792]{1,0:T(8,128)}) custom-call(bf16[256,4096]{1,0:T(8,128)(2,1)} %tokens.1, bf16[256,1792]{1,0:T(8,128)(2,1)} %gate.1, f32[128,1792]{1,0:T(8,128)} %latent.1, bf16[256,1792]{1,0:T(8,128)(2,1)} %cot.1), custom_call_target="tpu_custom_call" | custom-call | tf_op jit(solution)/shard_map/pallas_call | solution.py:548
  165.1 0.0 copy-start.1
  165.1 0.0 copy-start.2
  165.1 0.0 copy-start
  165.1 2.3 %copy.12 = bf16[256,1792]{1,0:T(8,128)(2,1)} copy(bf16[256,1792]{1,0:T(8,128)(2,1)} %get-tuple-element.8) | data formatting | bytes 1835008
  167.4 0.0 copy-done.1
  167.4 0.9 copy.13
  168.3 0.0 copy-done.2
  168.3 0.7 copy.14
  169.0 0.0 copy-done
  169.0 0.9 copy.15
Async XLA Ops:
  165.1 2.3 %copy-start.1 = (bf16[256,1792]{1,0:T(8,128)(2,1)S(1)}, bf16[256,1792]{1,0:T(8,128)(2,1)}, u32[]{:S(2)}) copy-start(bf16[256,1792]{1,0:T(8,128)(2,1)} %get-tuple-element.9) | copy-start | bytes 2752516
  165.1 3.3 %copy-start.2 = (bf16[256,512]{1,0:T(8,128)(2,1)S(1)}, bf16[256,512]{1,0:T(8,128)(2,1)}, u32[]{:S(2)}) copy-start(bf16[256,512]{1,0:T(8,128)(2,1)} %get-tuple-element.10) | copy-start | bytes 786436
  165.1 3.9 %copy-start = (f32[128,1792]{1,0:T(8,128)S(1)}, f32[128,1792]{1,0:T(8,128)}, u32[]{:S(2)}) copy-start(f32[128,1792]{1,0:T(8,128)} %get-tuple-element.11) | copy-start | bytes 2752516

commit v2 on v1

v2 whole, which is shorter than its diff:
```python
import functools

import jax
import jax.numpy as jnp
from jax import lax
from jax.experimental import pallas as pl
from jax.experimental.pallas import tpu as pltpu
from jax.sharding import PartitionSpec as P

D = 4096
FF = 14336
TOK = 256
COLS = 1792
HALF = COLS // 2
ROWS = 128
BLOCK = 1024
EPSILON = 1e-05
MESH = pl.DeviceIdType.MESH
F32 = jnp.float32
BF16 = jnp.bfloat16


def kernel(
    tokens, gate, latent, cot,
    hidden_out, gate_out, token_out, up_out,
    lat32, wg, wt, tokg, tokt, ucg, gate_v, cot_v, fa, fb,
    gp, gxs, gxr, gsend, grl, grr,
    pvf, pvs, fwd, chain, direct,
    tt_own, tt_send, tt_recv, zsend, zrecv, fsend, tgr,
    s1, s2, s3,
    in_sem, zr_sem, zsr_sem, zsl_sem, cs_sem, cr_sem,
    yrs, yrr, yls, ylr, tks, tkr, txs, txr,
    s1s, s1r, s2s, s2r, s3s, s3r,
    gcs, gcr, gls, glr, grs, grr_sem,
    ops, opr, tts, ttr, zxs, zxr, fs, fr,
):
    me_dp = lax.axis_index("dp")
    me_t = lax.axis_index("tensor")
    y = me_dp // 8
    g8 = me_dp % 8
    zl = g8 // 2
    k = g8 % 2
    x = me_t % 4
    zh = me_t // 4

    def dp_of(yy, zz, kk):
        return yy * 8 + zz * 2 + kk

    def at_y(d):
        return (((y + d) % 4) * 8 + g8, me_t)

    def at_z(zz):
        return (dp_of(y, zz, k), me_t)

    other = (dp_of(y, zl, 1 - k), me_t)

    def at_x(d):
        return (me_dp, zh * 4 + (x + d) % 4)

    flip = (me_dp, (1 - zh) * 4 + x)

    def rcopy(src, dst, ssem, rsem, dev):
        return pltpu.make_async_remote_copy(
            src_ref=src, dst_ref=dst, send_sem=ssem, recv_sem=rsem,
            device_id=dev, device_id_type=MESH,
        )

    source_x, source_y = y, 2 * zh + x // 2
    self_source = jnp.logical_and(source_x == x, source_y == y)
    collects = zh == y // 2

    def final_dev(j):
        return (dp_of(x, zl, k), zh * 4 + 2 * (y % 2) + j)

    def final_self(j):
        return jnp.logical_and(x == y, 2 * (y % 2) + j == x)

    def span(start, size):
        return pl.ds(pl.multiple_of(start, size), size)

    lat_in = pltpu.make_async_copy(latent, lat32, in_sem.at[0])
    gate_in = pltpu.make_async_copy(gate, gate_v, in_sem.at[1])
    cot_in = pltpu.make_async_copy(cot, cot_v, in_sem.at[2])
    tok_in = pltpu.make_async_copy(
        tokens.at[:, span(y * BLOCK, BLOCK)], tokg.at[span(y * TOK, TOK)], in_sem.at[3]
    )
    lat_in.start()
    gate_in.start()
    cot_in.start()
    tok_in.start()

    barrier = pltpu.get_barrier_semaphore()

    def greet(dev):
        pl.semaphore_signal(barrier, inc=1, device_id=dev, device_id_type=MESH)

    for d in range(1, 4):
        greet(at_y(d))
    for d in range(1, 8):
        greet((y * 8 + (g8 + d) % 8, me_t))
        greet((me_dp, (me_t + d) % 8))

    @pl.when(jnp.logical_not(self_source))
    def _():
        greet((dp_of(source_y, zl, k), zh * 4 + source_x))

    takers = jnp.int32(2)
    for j in range(2):
        takers = takers - jnp.where(final_self(j), 1, 0)
    pl.semaphore_wait(barrier, 17 + jnp.where(collects, takers, 0))

    def tok_send(d):
        yy = (y + d) % 4
        return rcopy(
            tokens.at[span(x * 64, 64), span(yy * BLOCK, BLOCK)],
            tokg.at[span(y * TOK + x * 64, 64)],
            tks.at[d], tkr.at[d], at_y(d),
        )

    def tok_share(d, e):
        piece = tokg.at[span(((y + 4 - d) % 4) * TOK + x * 64, 64)]
        return rcopy(piece, piece, txs.at[d, e], txr.at[d, e], at_x(e))

    for d in (1, 3, 2):
        tok_send(d).start()

    lat_in.wait()

    def cast_rows(i, acc):
        rows = span(i * 16, 16)
        half = lat32[rows, :].astype(BF16)
        wg[zl, k, rows, :] = half
        mag = jnp.abs(half.astype(F32))
        mag = mag[0:8] + mag[8:16]
        tot = mag[:, 0:128]
        for c in range(1, COLS // 128):
            tot = tot + mag[:, c * 128:(c + 1) * 128]
        return acc + tot

    part = lax.fori_loop(0, ROWS // 16, cast_rows, jnp.zeros((8, 128), F32))

    def z_right(b):
        return rcopy(wg.at[b, k], wg.at[b, k], zsr_sem.at[b], zr_sem.at[b], at_z(lax.rem(zl + 1, 4)))

    def z_left(b):
        return rcopy(wg.at[b, k], wg.at[b, k], zsl_sem.at[b], zr_sem.at[b], at_z(lax.rem(zl + 3, 4)))

    def c_send(b):
        return rcopy(wg.at[b, k], wg.at[b, k], cs_sem.at[b], cr_sem.at[b], other)

    def c_recv(b):
        return rcopy(wg.at[b, k], wg.at[b, 1 - k], cs_sem.at[b], cr_sem.at[b], other)

    @pl.when(zl < 3)
    def _():
        z_right(zl).start()

    @pl.when(zl > 0)
    def _():
        z_left(zl).start()

    c_send(zl).start()

    s1[g8] = part

    def s1_copy(d):
        return rcopy(s1.at[g8], s1.at[g8], s1s.at[d], s1r.at[d], (y * 8 + (g8 + d) % 8, me_t))

    def s2_copy(d):
        return rcopy(s2.at[y], s2.at[y], s2s.at[d], s2r.at[d], at_y(d))

    def s3_copy(d):
        return rcopy(s3.at[me_t], s3.at[me_t], s3s.at[d], s3r.at[d], (me_dp, (me_t + d) % 8))

    for d in range(1, 8):
        s1_copy(d).start()

    gate_in.wait()
    cot_in.wait()

    def cot_rows(lo, hi):
        @pl.loop(lo // 16, hi // 16)
        def _(i):
            rows = span(i * 16, 16)
            g = gate_v[rows, :].astype(F32)
            act = g * jax.nn.sigmoid(g)
            ucg[span(y * TOK + i * 16, 16), :] = (cot_v[rows, :].astype(F32) * act).astype(BF16)

    def cols(h):
        return pl.ds(h * HALF, HALF)

    def uc_part(yy, rows, h):
        return ucg.at[span((yy % 4) * TOK + rows * 128, 128), cols(h)]

    def y_right(h, i):
        piece = (uc_part(y, 0, h), uc_part(y, 1, h), uc_part(y + 3, 0, h))[i]
        return rcopy(piece, piece, yrs.at[h, i], yrr.at[h, i], at_y(1))

    def y_left(h, i):
        piece = (uc_part(y, 1, h), uc_part(y, 0, h), uc_part(y + 1, 1, h))[i]
        return rcopy(piece, piece, yls.at[h, i], ylr.at[h, i], at_y(3))

    def y_start(h):
        y_right(h, 0).start()
        y_left(h, 0).start()
        y_right(h, 1).start()
        y_left(h, 1).start()

    def y_pass(h):
        y_right(h, 0).wait_recv()
        y_right(h, 2).start()
        y_left(h, 0).wait_recv()
        y_left(h, 2).start()

    def y_wait(h, i):
        y_right(h, i).wait_recv()
        y_left(h, i).wait_recv()

    cot_rows(0, 256)
    y_start(0)

    for d in (1, 3, 2):
        tok_send(d).wait_recv()
        for e in (2, 1, 3):
            tok_share(d, e).start()

    for d in range(1, 8):
        s1_copy(d).wait_recv()
    tot = s1[0]
    for i in range(1, 8):
        tot = tot + s1[i]
    s2[y] = tot
    for d in range(1, 4):
        s2_copy(d).start()

    def at_distance(s, do):
        @pl.when(zl - s >= 0)
        def _():
            do(lax.rem(zl - s + 4, 4), True)

        @pl.when(zl + s <= 3)
        def _():
            do(lax.rem(zl + s, 4), False)

    def z_pass(b, from_left):
        if from_left:
            z_right(b).wait_recv()

            @pl.when(zl < 3)
            def _():
                z_right(b).start()
        else:
            z_left(b).wait_recv()

            @pl.when(zl > 0)
            def _():
                z_left(b).start()

        c_send(b).start()

    y_pass(0)
    y_start(1)
    at_distance(1, z_pass)
    for d in range(1, 4):
        s2_copy(d).wait_recv()
    tot = s2[0]
    for i in range(1, 4):
        tot = tot + s2[i]
    s3[me_t] = tot
    for d in range(1, 8):
        s3_copy(d).start()

    @pl.loop(0, TOK // 16)
    def _(i):
        rows = span(i * 16, 16)
        g = gate_v[rows, :].astype(F32)
        sig = jax.nn.sigmoid(g)
        fa[rows, :] = g * sig
        fb[rows, :] = cot_v[rows, :].astype(F32) * sig * (1.0 + g * (1.0 - sig))

    for d in range(1, 8):
        s3_copy(d).wait_recv()
    tot = s3[0]
    for i in range(1, 8):
        tot = tot + s3[i]
    total = jnp.sum(jnp.sum(tot, axis=0, keepdims=True), axis=1, keepdims=True)
    scale = total / (D * FF) + EPSILON
    bound = 0.5 * scale
    plus = scale.astype(BF16).astype(F32)

    def tern(b, from_left=None):
        c_recv(b).wait_recv()

        @pl.loop(0, 16)
        def _(i):
            wide = wg[b, i // 8, span((i % 8) * 16, 16), :].astype(F32)
            value = jnp.where(wide > bound, plus, jnp.where(wide < -bound, -plus, 0.0))
            wt[span(b * 256 + i * 16, 16), :] = value.astype(BF16)

    def m3(yy, half):
        yy = yy % 4
        d = (yy + 4 - x) % 4
        tt_send[d, half] = lax.dot_general(
            ucg[span(yy * TOK, TOK), :], wt[span(half * 512, 512), :],
            (((1,), (1,)), ((), ())), preferred_element_type=F32,
        ).astype(BF16)

        @pl.when(d > 0)
        def _():
            t_send(d, half).start()

    def t_send(d, half):
        return rcopy(tt_send.at[d, half], tt_recv.at[d, half], tts.at[d, half], ttr.at[d, half], at_x(d))

    early, late = zl // 2, 1 - zl // 2

    tern(zl)
    at_distance(1, tern)
    y_wait(0, 1)
    y_wait(0, 2)
    at_distance(2, z_pass)
    at_distance(2, tern)

    tok_in.wait()
    for d in (1, 3, 2):
        for e in (2, 1, 3):
            tok_share(d, e).wait_recv()
    for b in range(4):
        tokt[b, 0:128, :] = tokg[:, span(b * 256 + k * 128, 128)].T
        tokt[b, 128:256, :] = tokg[:, span(b * 256 + (1 - k) * 128, 128)].T

    def m1(target, h):
        term = jnp.dot(tokt[target], ucg[:, cols(h)], preferred_element_type=F32)
        gp[target, :, cols(h)] = term[0:128]
        gxs[target, :, cols(h)] = term[128:256].astype(BF16)
        g_cross(target, h).start()

    def part_of(ref, target, h):
        return ref.at[target, :, cols(h)]

    def g_cross(target, h):
        return rcopy(part_of(gxs, target, h), part_of(gxr, target, h), gcs.at[target, h], gcr.at[target, h], other)

    def g_right(target, h):
        return rcopy(
            part_of(gsend, target, h), part_of(grl, target, h),
            grs.at[target, h], glr.at[target, h], at_z(lax.rem(zl + 1, 4)),
        )

    def g_left(target, h):
        return rcopy(
            part_of(gsend, target, h), part_of(grr, target, h),
            gls.at[target, h], grr_sem.at[target, h], at_z(lax.rem(zl + 3, 4)),
        )

    def add_up(target, h, extra):
        @pl.loop(0, ROWS // 16)
        def _(i):
            rows = span(i * 16, 16)
            value = gp[target, rows, cols(h)] + gxr[target, rows, cols(h)].astype(F32)
            if extra is not None:
                value = value + extra[target, rows, cols(h)].astype(F32)
            gsend[target, rows, cols(h)] = value.astype(BF16)

    def combine(target, h):
        g_cross(target, h).wait_recv()

        @pl.when(target > zl)
        def _():
            @pl.when(zl == 0)
            def _():
                add_up(target, h, None)

            @pl.when(zl > 0)
            def _():
                g_right(target, h).wait_recv()
                add_up(target, h, grl)

            g_right(target, h).start()

        @pl.when(target < zl)
        def _():
            @pl.when(zl == 3)
            def _():
                add_up(target, h, None)

            @pl.when(zl < 3)
            def _():
                g_left(target, h).wait_recv()
                add_up(target, h, grr)

            g_left(target, h).start()

    def pick(a0, a1, a2, a3):
        return jnp.where(zl == 0, a0, jnp.where(zl == 1, a1, jnp.where(zl == 2, a2, a3)))

    order = [pick(3, 3, 0, 0), pick(2, 0, 3, 1), pick(1, 2, 1, 2), zl]
    edge = jnp.logical_or(zl == 0, zl == 3)

    def m2(yy, first, second):
        term = jnp.dot(tokg[span((yy % 4) * TOK, TOK), :], wt[...], preferred_element_type=F32)
        first[0:128, :] = term[0:128].astype(first.dtype)
        second[128:256, :] = term[128:256].astype(second.dtype)

    A, B = pl.ds(0, 128), pl.ds(128, 128)

    def p_minus(i):
        slot, rows = ((0, A), (1, B), (1, A))[i]
        dst = (fwd, direct, chain)[i]
        return rcopy(pvs.at[slot, rows], dst.at[rows], ops.at[0, i], opr.at[0, i], at_y(3))

    def p_plus(i):
        slot, rows = ((0, B), (2, A), (2, B))[i]
        dst = (fwd, direct, chain)[i]
        return rcopy(pvs.at[slot, rows], dst.at[rows], ops.at[1, i], opr.at[1, i], at_y(1))

    def opposite():
        m2(y + 2, pvs.at[0], pvs.at[0])
        p_minus(0).start()
        p_plus(0).start()

    def ends(i, h):
        @pl.when(edge)
        def _():
            combine(order[i], h)

    def middle(i, h):
        @pl.when(jnp.logical_not(edge))
        def _():
            combine(order[i], h)

    m1(order[0], 0)
    ends(0, 0)
    y_pass(1)
    m1(order[1], 0)
    ends(1, 0)
    m1(order[2], 0)
    ends(2, 0)
    m1(order[3], 0)
    m3(y, early)
    y_wait(1, 1)
    m3(y + 1, early)
    m3(y + 3, early)
    middle(0, 0)
    at_distance(3, z_pass)
    at_distance(3, tern)
    opposite()
    y_wait(1, 2)
    m1(order[0], 1)
    ends(0, 1)
    m3(y + 2, early)
    middle(2, 0)
    m2(y + 3, pvf.at[1], pvs.at[1])
    p_minus(1).start()
    m2(y + 1, pvs.at[2], pvf.at[1])
    p_plus(1).start()
    middle(1, 0)
    m1(order[1], 1)
    ends(1, 1)
    m1(order[2], 1)
    ends(2, 1)
    m1(order[3], 1)
    for d in range(4):
        m3(y + d, late)

    def z_copy(half):
        return rcopy(zsend.at[half], zrecv.at[half], zxs.at[half], zxr.at[half], flip)

    def sum_x(half):
        for d in range(1, 4):
            t_send(d, half).wait_recv()

        @pl.loop(0, TOK // 16)
        def _(i):
            rows = span(i * 16, 16)
            total = tt_send[0, half, rows, :].astype(F32)
            for d in range(1, 4):
                total = total + tt_recv[d, half, rows, :].astype(F32)
            tt_own[half, rows, :] = total
            zsend[half, rows, :] = total.astype(BF16)

        @pl.when(jnp.logical_not(collects))
        def _():
            z_copy(half).start()

    def f_send(half):
        return rcopy(fsend.at[half], tgr, fs.at[half], fr, final_dev(half))

    def sum_z(half):
        @pl.when(collects)
        def _():
            z_copy(half).wait_recv()

            @pl.loop(0, TOK // 16)
            def _(i):
                rows = span(i * 16, 16)
                fsend[half, rows, :] = (tt_own[half, rows, :] + zrecv[half, rows, :].astype(F32)).astype(BF16)

            @pl.when(jnp.logical_not(final_self(half)))
            def _():
                f_send(half).start()

            @pl.when(final_self(half))
            def _():
                tgr[...] = fsend[half]

    sum_x(early)
    middle(0, 1)

    def add_fwd(slot, h):
        @pl.loop(h * 8, h * 8 + 8)
        def _(i):
            rows = span(i * 16, 16)
            pvs[slot, rows, :] = (pvf[1, rows, :] + fwd[rows, :].astype(F32)).astype(BF16)

    p_minus(0).wait_recv()
    add_fwd(1, 0)
    p_minus(2).start()
    p_plus(0).wait_recv()
    add_fwd(2, 1)
    p_plus(2).start()
    m2(y, pvf.at[0], pvf.at[0])
    middle(2, 1)
    middle(1, 1)
    sum_x(late)
    sum_z(early)

    def finish(h):
        @pl.loop(h * 8, h * 8 + 8)
        def _(i):
            rows = span(i * 16, 16)
            up = pvf[0, rows, :] + chain[rows, :].astype(F32) + direct[rows, :].astype(F32)
            hidden_out[rows, :] = (fa[rows, :] * up).astype(BF16)
            gate_out[rows, :] = (fb[rows, :] * up).astype(BF16)

    p_plus(1).wait_recv()
    p_minus(2).wait_recv()
    finish(0)
    p_minus(1).wait_recv()
    p_plus(2).wait_recv()
    finish(1)

    sum_z(late)

    for h in range(2):
        g_cross(zl, h).wait_recv()
        up_out[:, cols(h)] = gp[zl, :, cols(h)] + gxr[zl, :, cols(h)].astype(F32)

        @pl.when(zl > 0)
        def _():
            g_right(zl, h).wait_recv()
            up_out[:, cols(h)] += grl[zl, :, cols(h)].astype(F32)

        @pl.when(zl < 3)
        def _():
            g_left(zl, h).wait_recv()
            up_out[:, cols(h)] += grr[zl, :, cols(h)].astype(F32)

    @pl.when(jnp.logical_not(self_source))
    def _():
        f_send(0).wait_recv()

    token_out[...] = tgr[...]

    for d in range(1, 4):
        tok_send(d).wait_send()
        s2_copy(d).wait_send()
        t_send(d, 0).wait_send()
        t_send(d, 1).wait_send()
        for e in range(1, 4):
            tok_share(d, e).wait_send()
    for d in range(1, 8):
        s1_copy(d).wait_send()
        s3_copy(d).wait_send()
    for i in range(3):
        for h in range(2):
            y_right(h, i).wait_send()
            y_left(h, i).wait_send()
        p_minus(i).wait_send()
        p_plus(i).wait_send()
    for b in range(4):
        c_send(b).wait_send()
        g_cross(b, 0).wait_send()
        g_cross(b, 1).wait_send()

        @pl.when(jnp.logical_and(zl < 3, b <= zl))
        def _():
            z_right(b).wait_send()

        @pl.when(jnp.logical_and(zl > 0, b >= zl))
        def _():
            z_left(b).wait_send()

        @pl.when(b > zl)
        def _():
            g_right(b, 0).wait_send()
            g_right(b, 1).wait_send()

        @pl.when(b < zl)
        def _():
            g_left(b, 0).wait_send()
            g_left(b, 1).wait_send()

    @pl.when(jnp.logical_not(collects))
    def _():
        z_copy(0).wait_send()
        z_copy(1).wait_send()

    for j in range(2):
        @pl.when(jnp.logical_and(collects, jnp.logical_not(final_self(j))))
        def _():
            f_send(j).wait_send()


def on_device(tokens, gate_values, up_latent, hidden_grad):
    dma = pltpu.SemaphoreType.DMA
    vm = pltpu.VMEM
    return pl.pallas_call(
        kernel,
        out_shape=(
            jax.ShapeDtypeStruct((TOK, COLS), BF16),
            jax.ShapeDtypeStruct((TOK, COLS), BF16),
            jax.ShapeDtypeStruct((TOK, 512), BF16),
            jax.ShapeDtypeStruct((ROWS, COLS), F32),
        ),
        in_specs=[pl.BlockSpec(memory_space=pl.ANY)] * 4,
        out_specs=(pl.BlockSpec(memory_space=pltpu.VMEM),) * 4,
        scratch_shapes=[
            vm((ROWS, COLS), F32),
            vm((4, 2, ROWS, COLS), BF16),
            vm((BLOCK, COLS), BF16),
            vm((BLOCK, BLOCK), BF16),
            vm((4, 256, BLOCK), BF16),
            vm((BLOCK, COLS), BF16),
            vm((TOK, COLS), BF16),
            vm((TOK, COLS), BF16),
            vm((TOK, COLS), F32),
            vm((TOK, COLS), F32),
            vm((4, ROWS, COLS), F32),
            vm((4, ROWS, COLS), BF16),
            vm((4, ROWS, COLS), BF16),
            vm((4, ROWS, COLS), BF16),
            vm((4, ROWS, COLS), BF16),
            vm((4, ROWS, COLS), BF16),
            vm((2, TOK, COLS), F32),
            vm((3, TOK, COLS), BF16),
            vm((TOK, COLS), BF16),
            vm((TOK, COLS), BF16),
            vm((TOK, COLS), BF16),
            vm((2, TOK, 512), F32),
            vm((4, 2, TOK, 512), BF16),
            vm((4, 2, TOK, 512), BF16),
            vm((2, TOK, 512), BF16),
            vm((2, TOK, 512), BF16),
            vm((2, TOK, 512), BF16),
            vm((TOK, 512), BF16),
            vm((8, 8, 128), F32),
            vm((4, 8, 128), F32),
            vm((8, 8, 128), F32),
            dma((4,)),
            dma((4,)), dma((4,)), dma((4,)), dma((4,)), dma((4,)),
            dma((2, 3)), dma((2, 3)), dma((2, 3)), dma((2, 3)), dma((4,)), dma((4,)), dma((4, 4)), dma((4, 4)),
            dma((8,)), dma((8,)), dma((4,)), dma((4,)), dma((8,)), dma((8,)),
            dma((4, 2)), dma((4, 2)), dma((4, 2)), dma((4, 2)), dma((4, 2)), dma((4, 2)),
            dma((2, 3)), dma((2, 3)), dma((4, 2)), dma((4, 2)), dma((2,)), dma((2,)), dma((2,)), dma,
        ],
        compiler_params=pltpu.CompilerParams(
            collective_id=0, has_side_effects=True, vmem_limit_bytes=60 * 1024 * 1024
        ),
    )(tokens, gate_values, up_latent, hidden_grad)


def solution(mesh):
    placed = (P("dp", None), P("dp", "tensor"), P("dp", "tensor"), P("dp", "tensor"))
    return jax.shard_map(
        on_device,
        mesh=mesh,
        in_specs=placed,
        out_specs=(P("dp", "tensor"), P("dp", "tensor"), P("dp", "tensor"), P("dp", "tensor")),
        check_vma=False,
    )
```

time: 170 us -> 116 us (0.68)
  the two profiles are of different devices: /device:TPU:56 before, /device:TPU:62 now
where the time goes in v2:
time: 116 us
  Pallas kernels  111 us (96%)
  local copies, waits for them, and re-layouts  4.87 us (4%)
    pallas_call x1, Pallas kernels, on_device(): pl.pallas_call(kernel, out_shape=(jax.ShapeDtypeStruct((TOK, COLS), BF16)...  111 us
    unnamed x10, local copies, waits for them, and re-layouts  4.87 us

profile of v2, /device:TPU:62, one launch (start us, length us, event | category | flops | bytes accessed | tf_op | source)
XLA Modules:
  0.0 116.2 jit_solution(4669553354107178003)
XLA Ops:
  0.6 110.7 %shard_map.75 = (bf16[256,1792]{1,0:T(8,128)(2,1)}, bf16[256,1792]{1,0:T(8,128)(2,1)}, bf16[256,512]{1,0:T(8,128)(2,1)}, f32[128,1792]{1,0:T(8,128)}) custom-call(bf16[256,4096]{1,0:T(8,128)(2,1)} %tokens.1, bf16[256,1792]{1,0:T(8,128)(2,1)} %gate.1, f32[128,1792]{1,0:T(8,128)} %latent.1, bf16[256,1792]{1,0:T(8,128)(2,1)} %cot.1), custom_call_target="tpu_custom_call" | custom-call | tf_op jit(solution)/shard_map/pallas_call | solution.py:618
  111.3 0.0 copy-start.1
  111.3 0.0 copy-start.2
  111.3 0.0 copy-start
  111.3 2.3 %copy.12 = bf16[256,1792]{1,0:T(8,128)(2,1)} copy(bf16[256,1792]{1,0:T(8,128)(2,1)} %get-tuple-element.8) | data formatting | bytes 1835008
  113.6 0.0 copy-done.1
  113.6 0.9 copy.13
  114.6 0.0 copy-done.2
  114.6 0.7 copy.14
  115.3 0.0 copy-done
  115.3 0.9 copy.15
Async XLA Ops:
  111.3 2.3 %copy-start.1 = (bf16[256,1792]{1,0:T(8,128)(2,1)S(1)}, bf16[256,1792]{1,0:T(8,128)(2,1)}, u32[]{:S(2)}) copy-start(bf16[256,1792]{1,0:T(8,128)(2,1)} %get-tuple-element.9) | copy-start | bytes 2752516
  111.3 3.3 %copy-start.2 = (bf16[256,512]{1,0:T(8,128)(2,1)S(1)}, bf16[256,512]{1,0:T(8,128)(2,1)}, u32[]{:S(2)}) copy-start(bf16[256,512]{1,0:T(8,128)(2,1)} %get-tuple-element.10) | copy-start | bytes 786436
  111.3 3.9 %copy-start = (f32[128,1792]{1,0:T(8,128)S(1)}, f32[128,1792]{1,0:T(8,128)}, u32[]{:S(2)}) copy-start(f32[128,1792]{1,0:T(8,128)} %get-tuple-element.11) | copy-start | bytes 2752516

commit v3 on v2

--- a/solution.py
+++ b/solution.py
@@ -26,7 +26,7 @@
     lat32, wg, wt, tokg, tokt, ucg, gate_v, cot_v, fa, fb,
     gp, gxs, gxr, gsend, grl, grr,
     pvf, pvs, fwd, chain, direct,
-    tt_own, tt_send, tt_recv, zsend, zrecv, fsend, tgr,
+    tt_send, tt_recv, tt_own, zsend, zrecv, fsend, tgr,
     s1, s2, s3,
     in_sem, zr_sem, zsr_sem, zsl_sem, cs_sem, cr_sem,
     yrs, yrr, yls, ylr, tks, tkr, txs, txr,
@@ -65,15 +65,17 @@
             device_id=dev, device_id_type=MESH,
         )
 
-    source_x, source_y = y, 2 * zh + x // 2
-    self_source = jnp.logical_and(source_x == x, source_y == y)
+    source_y = 2 * zh + x // 2
     collects = zh == y // 2
 
-    def final_dev(j):
-        return (dp_of(x, zl, k), zh * 4 + 2 * (y % 2) + j)
-
-    def final_self(j):
-        return jnp.logical_and(x == y, 2 * (y % 2) + j == x)
+    def final_dev(yy, half):
+        return (dp_of(yy, zl, k), zh * 4 + 2 * (y % 2) + half)
+
+    def final_self(yy, half):
+        return jnp.logical_and(yy == y, 2 * (y % 2) + half == x)
+
+    def source_self(xx):
+        return jnp.logical_and(source_y == y, xx == x)
 
     def span(start, size):
         return pl.ds(pl.multiple_of(start, size), size)
@@ -100,13 +102,15 @@
         greet((y * 8 + (g8 + d) % 8, me_t))
         greet((me_dp, (me_t + d) % 8))
 
-    @pl.when(jnp.logical_not(self_source))
-    def _():
-        greet((dp_of(source_y, zl, k), zh * 4 + source_x))
-
-    takers = jnp.int32(2)
-    for j in range(2):
-        takers = takers - jnp.where(final_self(j), 1, 0)
+    for xx in range(4):
+        @pl.when(jnp.logical_not(source_self(xx)))
+        def _():
+            greet((dp_of(source_y, zl, k), zh * 4 + xx))
+
+    takers = jnp.int32(8)
+    for yy in range(4):
+        for half in range(2):
+            takers = takers - jnp.where(final_self(yy, half), 1, 0)
     pl.semaphore_wait(barrier, 17 + jnp.where(collects, takers, 0))
 
     def tok_send(d):
@@ -151,6 +155,20 @@
     def c_recv(b):
         return rcopy(wg.at[b, k], wg.at[b, 1 - k], cs_sem.at[b], cr_sem.at[b], other)
 
+    s1[g8] = part
+
+    def s1_copy(d):
+        return rcopy(s1.at[g8], s1.at[g8], s1s.at[d], s1r.at[d], (y * 8 + (g8 + d) % 8, me_t))
+
+    def s2_copy(d):
+        return rcopy(s2.at[y], s2.at[y], s2s.at[d], s2r.at[d], at_y(d))
+
+    def s3_copy(d):
+        return rcopy(s3.at[me_t], s3.at[me_t], s3s.at[d], s3r.at[d], (me_dp, (me_t + d) % 8))
+
+    for d in range(1, 8):
+        s1_copy(d).start()
+
     @pl.when(zl < 3)
     def _():
         z_right(zl).start()
@@ -161,19 +179,6 @@
 
     c_send(zl).start()
 
-    s1[g8] = part
-
-    def s1_copy(d):
-        return rcopy(s1.at[g8], s1.at[g8], s1s.at[d], s1r.at[d], (y * 8 + (g8 + d) % 8, me_t))
-
-    def s2_copy(d):
-        return rcopy(s2.at[y], s2.at[y], s2s.at[d], s2r.at[d], at_y(d))
-
-    def s3_copy(d):
-        return rcopy(s3.at[me_t], s3.at[me_t], s3s.at[d], s3r.at[d], (me_dp, (me_t + d) % 8))
-
-    for d in range(1, 8):
-        s1_copy(d).start()
 
     gate_in.wait()
     cot_in.wait()
@@ -219,56 +224,17 @@
     cot_rows(0, 256)
     y_start(0)
 
-    for d in (1, 3, 2):
-        tok_send(d).wait_recv()
-        for e in (2, 1, 3):
-            tok_share(d, e).start()
-
-    for d in range(1, 8):
-        s1_copy(d).wait_recv()
-    tot = s1[0]
-    for i in range(1, 8):
-        tot = tot + s1[i]
-    s2[y] = tot
+    def reduced(slots, copy, n):
+        for d in range(1, n):
+            copy(d).wait_recv()
+        tot = slots[0]
+        for i in range(1, n):
+            tot = tot + slots[i]
+        return tot
+
+    s2[y] = reduced(s1, s1_copy, 8)
     for d in range(1, 4):
         s2_copy(d).start()
-
-    def at_distance(s, do):
-        @pl.when(zl - s >= 0)
-        def _():
-            do(lax.rem(zl - s + 4, 4), True)
-
-        @pl.when(zl + s <= 3)
-        def _():
-            do(lax.rem(zl + s, 4), False)
-
-    def z_pass(b, from_left):
-        if from_left:
-            z_right(b).wait_recv()
-
-            @pl.when(zl < 3)
-            def _():
-                z_right(b).start()
-        else:
-            z_left(b).wait_recv()
-
-            @pl.when(zl > 0)
-            def _():
-                z_left(b).start()
-
-        c_send(b).start()
-
-    y_pass(0)
-    y_start(1)
-    at_distance(1, z_pass)
-    for d in range(1, 4):
-        s2_copy(d).wait_recv()
-    tot = s2[0]
-    for i in range(1, 4):
-        tot = tot + s2[i]
-    s3[me_t] = tot
-    for d in range(1, 8):
-        s3_copy(d).start()
 
     @pl.loop(0, TOK // 16)
     def _(i):
@@ -278,56 +244,53 @@
         fa[rows, :] = g * sig
         fb[rows, :] = cot_v[rows, :].astype(F32) * sig * (1.0 + g * (1.0 - sig))
 
+    for d in (1, 3, 2):
+        tok_send(d).wait_recv()
+        for e in (2, 1, 3):
+            tok_share(d, e).start()
+
+    def at_distance(s, do):
+        @pl.when(zl - s >= 0)
+        def _():
+            do(lax.rem(zl - s + 4, 4), True)
+
+        @pl.when(zl + s <= 3)
+        def _():
+            do(lax.rem(zl + s, 4), False)
+
+    def z_pass(b, from_left):
+        if from_left:
+            z_right(b).wait_recv()
+
+            @pl.when(zl < 3)
+            def _():
+                z_right(b).start()
+        else:
+            z_left(b).wait_recv()
+
+            @pl.when(zl > 0)
+            def _():
+                z_left(b).start()
+
+        c_send(b).start()
+
+    at_distance(1, z_pass)
+    y_pass(0)
+    y_start(1)
+    s3[me_t] = reduced(s2, s2_copy, 4)
     for d in range(1, 8):
-        s3_copy(d).wait_recv()
-    tot = s3[0]
-    for i in range(1, 8):
-        tot = tot + s3[i]
-    total = jnp.sum(jnp.sum(tot, axis=0, keepdims=True), axis=1, keepdims=True)
-    scale = total / (D * FF) + EPSILON
-    bound = 0.5 * scale
-    plus = scale.astype(BF16).astype(F32)
-
-    def tern(b, from_left=None):
-        c_recv(b).wait_recv()
-
-        @pl.loop(0, 16)
-        def _(i):
-            wide = wg[b, i // 8, span((i % 8) * 16, 16), :].astype(F32)
-            value = jnp.where(wide > bound, plus, jnp.where(wide < -bound, -plus, 0.0))
-            wt[span(b * 256 + i * 16, 16), :] = value.astype(BF16)
-
-    def m3(yy, half):
-        yy = yy % 4
-        d = (yy + 4 - x) % 4
-        tt_send[d, half] = lax.dot_general(
-            ucg[span(yy * TOK, TOK), :], wt[span(half * 512, 512), :],
-            (((1,), (1,)), ((), ())), preferred_element_type=F32,
-        ).astype(BF16)
-
-        @pl.when(d > 0)
-        def _():
-            t_send(d, half).start()
-
-    def t_send(d, half):
-        return rcopy(tt_send.at[d, half], tt_recv.at[d, half], tts.at[d, half], ttr.at[d, half], at_x(d))
-
-    early, late = zl // 2, 1 - zl // 2
-
-    tern(zl)
-    at_distance(1, tern)
+        s3_copy(d).start()
+    at_distance(2, z_pass)
+    def turn(target):
+        tokt[target, 0:128, :] = tokg[:, span(target * 256 + k * 128, 128)].T
+        tokt[target, 128:256, :] = tokg[:, span(target * 256 + (1 - k) * 128, 128)].T
+
     y_wait(0, 1)
     y_wait(0, 2)
-    at_distance(2, z_pass)
-    at_distance(2, tern)
-
     tok_in.wait()
     for d in (1, 3, 2):
         for e in (2, 1, 3):
             tok_share(d, e).wait_recv()
-    for b in range(4):
-        tokt[b, 0:128, :] = tokg[:, span(b * 256 + k * 128, 128)].T
-        tokt[b, 128:256, :] = tokg[:, span(b * 256 + (1 - k) * 128, 128)].T
 
     def m1(target, h):
         term = jnp.dot(tokt[target], ucg[:, cols(h)], preferred_element_type=F32)
@@ -394,7 +357,7 @@
     def pick(a0, a1, a2, a3):
         return jnp.where(zl == 0, a0, jnp.where(zl == 1, a1, jnp.where(zl == 2, a2, a3)))
 
-    order = [pick(3, 3, 0, 0), pick(2, 0, 3, 1), pick(1, 2, 1, 2), zl]
+    order = [pick(3, 3, 0, 0), pick(2, 2, 1, 1), pick(1, 0, 3, 2), zl]
     edge = jnp.logical_or(zl == 0, zl == 3)
 
     def m2(yy, first, second):
@@ -429,83 +392,122 @@
         def _():
             combine(order[i], h)
 
+    turn(order[0])
     m1(order[0], 0)
+    turn(order[1])
+    m1(order[1], 0)
     ends(0, 0)
     y_pass(1)
-    m1(order[1], 0)
+    turn(order[2])
+    m1(order[2], 0)
     ends(1, 0)
-    m1(order[2], 0)
+    turn(order[3])
+    m1(order[3], 0)
     ends(2, 0)
-    m1(order[3], 0)
+
+    tot = reduced(s3, s3_copy, 8)
+    total = jnp.sum(jnp.sum(tot, axis=0, keepdims=True), axis=1, keepdims=True)
+    scale = total / (D * FF) + EPSILON
+    bound = 0.5 * scale
+    plus = scale.astype(BF16).astype(F32)
+
+    def tern(b, from_left=None):
+        c_recv(b).wait_recv()
+
+        @pl.loop(0, 16)
+        def _(i):
+            wide = wg[b, i // 8, span((i % 8) * 16, 16), :].astype(F32)
+            value = jnp.where(wide > bound, plus, jnp.where(wide < -bound, -plus, 0.0))
+            wt[span(b * 256 + i * 16, 16), :] = value.astype(BF16)
+
+    def m3(yy, half):
+        yy = yy % 4
+        tt_send[half, yy] = lax.dot_general(
+            ucg[span(yy * TOK, TOK), :], wt[span(half * 512, 512), :],
+            (((1,), (1,)), ((), ())), preferred_element_type=F32,
+        ).astype(BF16)
+        for d in (2, 1, 3):
+            t_send(yy, d, half).start()
+
+    def t_send(yy, d, half):
+        return rcopy(
+            tt_send.at[half, yy, span(((x + d) % 4) * 64, 64)], tt_recv.at[half, yy, d],
+            tts.at[half, yy, d], ttr.at[half, yy, d], at_x(d),
+        )
+
+    early, late = zl // 2, 1 - zl // 2
+
+    tern(zl)
+    at_distance(1, tern)
+    at_distance(2, tern)
+    at_distance(3, z_pass)
     m3(y, early)
     y_wait(1, 1)
     m3(y + 1, early)
     m3(y + 3, early)
-    middle(0, 0)
-    at_distance(3, z_pass)
     at_distance(3, tern)
     opposite()
+    m3(y, late)
+    m3(y + 1, late)
+    m3(y + 3, late)
+    middle(0, 0)
     y_wait(1, 2)
+    m3(y + 2, early)
+    m3(y + 2, late)
     m1(order[0], 1)
-    ends(0, 1)
-    m3(y + 2, early)
-    middle(2, 0)
     m2(y + 3, pvf.at[1], pvs.at[1])
     p_minus(1).start()
+    ends(0, 1)
     m2(y + 1, pvs.at[2], pvf.at[1])
     p_plus(1).start()
     middle(1, 0)
     m1(order[1], 1)
+    m1(order[2], 1)
     ends(1, 1)
-    m1(order[2], 1)
-    ends(2, 1)
-    m1(order[3], 1)
-    for d in range(4):
-        m3(y + d, late)
+    middle(2, 0)
 
     def z_copy(half):
         return rcopy(zsend.at[half], zrecv.at[half], zxs.at[half], zxr.at[half], flip)
 
+    def f_send(yy, half):
+        return rcopy(fsend.at[half, yy], tgr.at[span(x * 64, 64)], fs.at[half, yy], fr.at[x], final_dev(yy, half))
+
+    def f_recv(xx):
+        return rcopy(fsend.at[0, 0], tgr.at[span(xx * 64, 64)], fs.at[0, 0], fr.at[xx], final_dev(0, 0))
+
     def sum_x(half):
-        for d in range(1, 4):
-            t_send(d, half).wait_recv()
-
-        @pl.loop(0, TOK // 16)
-        def _(i):
-            rows = span(i * 16, 16)
-            total = tt_send[0, half, rows, :].astype(F32)
+        for i in (0, 1, 3, 2):
+            yy = (y + i) % 4
             for d in range(1, 4):
-                total = total + tt_recv[d, half, rows, :].astype(F32)
-            tt_own[half, rows, :] = total
-            zsend[half, rows, :] = total.astype(BF16)
+                t_send(yy, d, half).wait_recv()
+
+            @pl.loop(0, 4)
+            def _(r):
+                rows = span(r * 16, 16)
+                total = tt_send[half, yy, span(x * 64 + r * 16, 16), :].astype(F32)
+                for d in range(1, 4):
+                    total = total + tt_recv[half, yy, d, rows, :].astype(F32)
+                tt_own[half, yy, rows, :] = total
+                zsend[half, yy, rows, :] = total.astype(BF16)
 
         @pl.when(jnp.logical_not(collects))
         def _():
             z_copy(half).start()
-
-    def f_send(half):
-        return rcopy(fsend.at[half], tgr, fs.at[half], fr, final_dev(half))
 
     def sum_z(half):
         @pl.when(collects)
         def _():
             z_copy(half).wait_recv()
-
-            @pl.loop(0, TOK // 16)
-            def _(i):
-                rows = span(i * 16, 16)
-                fsend[half, rows, :] = (tt_own[half, rows, :] + zrecv[half, rows, :].astype(F32)).astype(BF16)
-
-            @pl.when(jnp.logical_not(final_self(half)))
-            def _():
-                f_send(half).start()
-
-            @pl.when(final_self(half))
-            def _():
-                tgr[...] = fsend[half]
-
-    sum_x(early)
-    middle(0, 1)
+            for yy in range(4):
+                fsend[half, yy] = (tt_own[half, yy] + zrecv[half, yy].astype(F32)).astype(BF16)
+
+                @pl.when(jnp.logical_not(final_self(yy, half)))
+                def _():
+                    f_send(yy, half).start()
+
+                @pl.when(final_self(yy, half))
+                def _():
+                    tgr[span(x * 64, 64), :] = fsend[half, yy]
 
     def add_fwd(slot, h):
         @pl.loop(h * 8, h * 8 + 8)
@@ -513,17 +515,22 @@
             rows = span(i * 16, 16)
             pvs[slot, rows, :] = (pvf[1, rows, :] + fwd[rows, :].astype(F32)).astype(BF16)
 
+    sum_x(early)
+    ends(2, 1)
+    m1(order[3], 1)
     p_minus(0).wait_recv()
     add_fwd(1, 0)
     p_minus(2).start()
     p_plus(0).wait_recv()
     add_fwd(2, 1)
     p_plus(2).start()
+    middle(0, 1)
+    sum_x(late)
     m2(y, pvf.at[0], pvf.at[0])
+    middle(1, 1)
+    sum_z(early)
     middle(2, 1)
-    middle(1, 1)
-    sum_x(late)
-    sum_z(early)
+    sum_z(late)
 
     def finish(h):
         @pl.loop(h * 8, h * 8 + 8)
@@ -540,8 +547,6 @@
     p_plus(2).wait_recv()
     finish(1)
 
-    sum_z(late)
-
     for h in range(2):
         g_cross(zl, h).wait_recv()
         up_out[:, cols(h)] = gp[zl, :, cols(h)] + gxr[zl, :, cols(h)].astype(F32)
@@ -556,17 +561,19 @@
             g_left(zl, h).wait_recv()
             up_out[:, cols(h)] += grr[zl, :, cols(h)].astype(F32)
 
-    @pl.when(jnp.logical_not(self_source))
-    def _():
-        f_send(0).wait_recv()
+    for xx in range(4):
+        @pl.when(jnp.logical_not(source_self(xx)))
+        def _():
+            f_recv(xx).wait_recv()
 
     token_out[...] = tgr[...]
 
     for d in range(1, 4):
         tok_send(d).wait_send()
         s2_copy(d).wait_send()
-        t_send(d, 0).wait_send()
-        t_send(d, 1).wait_send()
+        for b in range(4):
+            t_send(b, d, 0).wait_send()
+            t_send(b, d, 1).wait_send()
         for e in range(1, 4):
             tok_share(d, e).wait_send()
     for d in range(1, 8):
@@ -601,15 +608,15 @@
             g_left(b, 0).wait_send()
             g_left(b, 1).wait_send()
 
-    @pl.when(jnp.logical_not(collects))
-    def _():
-        z_copy(0).wait_send()
-        z_copy(1).wait_send()
-
-    for j in range(2):
-        @pl.when(jnp.logical_and(collects, jnp.logical_not(final_self(j))))
-        def _():
-            f_send(j).wait_send()
+    for half in range(2):
+        @pl.when(jnp.logical_not(collects))
+        def _():
+            z_copy(half).wait_send()
+
+        for yy in range(4):
+            @pl.when(jnp.logical_and(collects, jnp.logical_not(final_self(yy, half))))
+            def _():
+                f_send(yy, half).wait_send()
 
 
 def on_device(tokens, gate_values, up_latent, hidden_grad):
@@ -618,10 +625,10 @@
     return pl.pallas_call(
         kernel,
         out_shape=(
-            jax.ShapeDtypeStruct((TOK, COLS), BF16),
-            jax.ShapeDtypeStruct((TOK, COLS), BF16),
-            jax.ShapeDtypeStruct((TOK, 512), BF16),
-            jax.ShapeDtypeStruct((ROWS, COLS), F32),
+            vm((TOK, COLS), BF16),
+            vm((TOK, COLS), BF16),
+            vm((TOK, 512), BF16),
+            vm((ROWS, COLS), F32),
         ),
         in_specs=[pl.BlockSpec(memory_space=pl.ANY)] * 4,
         out_specs=(pl.BlockSpec(memory_space=pltpu.VMEM),) * 4,
@@ -647,12 +654,12 @@
             vm((TOK, COLS), BF16),
             vm((TOK, COLS), BF16),
             vm((TOK, COLS), BF16),
-            vm((2, TOK, 512), F32),
-            vm((4, 2, TOK, 512), BF16),
-            vm((4, 2, TOK, 512), BF16),
-            vm((2, TOK, 512), BF16),
-            vm((2, TOK, 512), BF16),
-            vm((2, TOK, 512), BF16),
+            vm((2, 4, TOK, 512), BF16),
+            vm((2, 4, 4, 64, 512), BF16),
+            vm((2, 4, 64, 512), F32),
+            vm((2, 4, 64, 512), BF16),
+            vm((2, 4, 64, 512), BF16),
+            vm((2, 4, 64, 512), BF16),
             vm((TOK, 512), BF16),
             vm((8, 8, 128), F32),
             vm((4, 8, 128), F32),
@@ -662,7 +669,7 @@
             dma((2, 3)), dma((2, 3)), dma((2, 3)), dma((2, 3)), dma((4,)), dma((4,)), dma((4, 4)), dma((4, 4)),
             dma((8,)), dma((8,)), dma((4,)), dma((4,)), dma((8,)), dma((8,)),
             dma((4, 2)), dma((4, 2)), dma((4, 2)), dma((4, 2)), dma((4, 2)), dma((4, 2)),
-            dma((2, 3)), dma((2, 3)), dma((4, 2)), dma((4, 2)), dma((2,)), dma((2,)), dma((2,)), dma,
+            dma((2, 3)), dma((2, 3)), dma((2, 4, 4)), dma((2, 4, 4)), dma((2,)), dma((2,)), dma((2, 4)), dma((4,)),
         ],
         compiler_params=pltpu.CompilerParams(
             collective_id=0, has_side_effects=True, vmem_limit_bytes=60 * 1024 * 1024

time: 116 us -> 103 us (0.89)
  the two profiles are of different devices: /device:TPU:62 before, /device:TPU:19 now
where the time goes in v3:
time: 103 us
  Pallas kernels  98.9 us (96%)
  local copies, waits for them, and re-layouts  3.47 us (3%)
    pallas_call x1, Pallas kernels, on_device(): pl.pallas_call(kernel, out_shape=(vm((TOK, COLS), BF16), vm((TOK, COLS),...  98.9 us
    unnamed x4, local copies, waits for them, and re-layouts  3.47 us

profile of v3, /device:TPU:19, one launch (start us, length us, event | category | flops | bytes accessed | tf_op | source)
XLA Modules:
  0.0 103.0 jit_solution(7194901050283549204)
XLA Ops:
  0.6 98.9 %shard_map.75 = (bf16[256,1792]{1,0:T(8,128)(2,1)S(1)}, bf16[256,1792]{1,0:T(8,128)(2,1)S(1)}, bf16[256,512]{1,0:T(8,128)(2,1)S(1)}, f32[128,1792]{1,0:T(8,128)S(1)}) custom-call(bf16[256,4096]{1,0:T(8,128)(2,1)} %tokens.1, bf16[256,1792]{1,0:T(8,128)(2,1)} %gate.1, f32[128,1792]{1,0:T(8,128)} %latent.1, bf16[256,1792]{1,0:T(8,128)(2,1)} %cot.1), custom_call_target="tpu_custom_call" | custom-call | tf_op jit(solution)/shard_map/pallas_call | solution.py:625
  99.5 0.9 copy.12
  100.4 0.7 copy.14
  101.1 0.9 copy.13
  102.1 0.9 copy.15

commit v4 on v3

--- a/solution.py
+++ b/solution.py
@@ -11,7 +11,7 @@
 FF = 14336
 TOK = 256
 COLS = 1792
-HALF = COLS // 2
+PARTS = ((0, 512), (512, 640), (1152, 640))
 ROWS = 128
 BLOCK = 1024
 EPSILON = 1e-05
@@ -26,7 +26,7 @@
     lat32, wg, wt, tokg, tokt, ucg, gate_v, cot_v, fa, fb,
     gp, gxs, gxr, gsend, grl, grr,
     pvf, pvs, fwd, chain, direct,
-    tt_send, tt_recv, tt_own, zsend, zrecv, fsend, tgr,
+    tt_send, tt_recv, zrecv, fsend, tgr,
     s1, s2, s3,
     in_sem, zr_sem, zsr_sem, zsl_sem, cs_sem, cr_sem,
     yrs, yrr, yls, ylr, tks, tkr, txs, txr,
@@ -65,17 +65,14 @@
             device_id=dev, device_id_type=MESH,
         )
 
-    source_y = 2 * zh + x // 2
-    collects = zh == y // 2
-
-    def final_dev(yy, half):
-        return (dp_of(yy, zl, k), zh * 4 + 2 * (y % 2) + half)
-
-    def final_self(yy, half):
-        return jnp.logical_and(yy == y, 2 * (y % 2) + half == x)
-
-    def source_self(xx):
-        return jnp.logical_and(source_y == y, xx == x)
+    def final_dev(yy, j):
+        return (dp_of(yy, zl, k), zh * 4 + 2 * (y % 2) + j)
+
+    def final_self(yy, j):
+        return jnp.logical_and(yy == y, 2 * (y % 2) + j == x)
+
+    def source_self(z, xx):
+        return jnp.logical_and(x // 2 + 2 * z == y, xx == x)
 
     def span(start, size):
         return pl.ds(pl.multiple_of(start, size), size)
@@ -102,16 +99,17 @@
         greet((y * 8 + (g8 + d) % 8, me_t))
         greet((me_dp, (me_t + d) % 8))
 
-    for xx in range(4):
-        @pl.when(jnp.logical_not(source_self(xx)))
-        def _():
-            greet((dp_of(source_y, zl, k), zh * 4 + xx))
+    for z in range(2):
+        for xx in range(4):
+            @pl.when(jnp.logical_not(source_self(z, xx)))
+            def _():
+                greet((dp_of(x // 2 + 2 * z, zl, k), zh * 4 + xx))
 
     takers = jnp.int32(8)
     for yy in range(4):
-        for half in range(2):
-            takers = takers - jnp.where(final_self(yy, half), 1, 0)
-    pl.semaphore_wait(barrier, 17 + jnp.where(collects, takers, 0))
+        for j in range(2):
+            takers = takers - jnp.where(final_self(yy, j), 1, 0)
+    pl.semaphore_wait(barrier, 17 + takers)
 
     def tok_send(d):
         yy = (y + d) % 4
@@ -121,9 +119,10 @@
             tks.at[d], tkr.at[d], at_y(d),
         )
 
-    def tok_share(d, e):
-        piece = tokg.at[span(((y + 4 - d) % 4) * TOK + x * 64, 64)]
-        return rcopy(piece, piece, txs.at[d, e], txr.at[d, e], at_x(e))
+    def tok_share(d, e, c):
+        half = zl // 2 if c else 1 - zl // 2
+        piece = tokg.at[span(((y + 4 - d) % 4) * TOK + x * 64, 64), span(half * 512, 512)]
+        return rcopy(piece, piece, txs.at[d - 1, e - 1, c], txr.at[d - 1, e - 1, c], at_x(e))
 
     for d in (1, 3, 2):
         tok_send(d).start()
@@ -192,7 +191,7 @@
             ucg[span(y * TOK + i * 16, 16), :] = (cot_v[rows, :].astype(F32) * act).astype(BF16)
 
     def cols(h):
-        return pl.ds(h * HALF, HALF)
+        return pl.ds(*PARTS[h])
 
     def uc_part(yy, rows, h):
         return ucg.at[span((yy % 4) * TOK + rows * 128, 128), cols(h)]
@@ -247,7 +246,10 @@
     for d in (1, 3, 2):
         tok_send(d).wait_recv()
         for e in (2, 1, 3):
-            tok_share(d, e).start()
+            tok_share(d, e, 0).start()
+    for d in (1, 3, 2):
+        for e in (2, 1, 3):
+            tok_share(d, e, 1).start()
 
     def at_distance(s, do):
         @pl.when(zl - s >= 0)
@@ -277,20 +279,14 @@
     at_distance(1, z_pass)
     y_pass(0)
     y_start(1)
-    s3[me_t] = reduced(s2, s2_copy, 4)
-    for d in range(1, 8):
-        s3_copy(d).start()
-    at_distance(2, z_pass)
     def turn(target):
         tokt[target, 0:128, :] = tokg[:, span(target * 256 + k * 128, 128)].T
         tokt[target, 128:256, :] = tokg[:, span(target * 256 + (1 - k) * 128, 128)].T
 
-    y_wait(0, 1)
-    y_wait(0, 2)
-    tok_in.wait()
-    for d in (1, 3, 2):
-        for e in (2, 1, 3):
-            tok_share(d, e).wait_recv()
+    def tok_wait(c):
+        for d in (1, 3, 2):
+            for e in (2, 1, 3):
+                tok_share(d, e, c).wait_recv()
 
     def m1(target, h):
         term = jnp.dot(tokt[target], ucg[:, cols(h)], preferred_element_type=F32)
@@ -392,18 +388,40 @@
         def _():
             combine(order[i], h)
 
+    y_wait(0, 1)
+    y_wait(0, 2)
+    tok_in.wait()
+    tok_wait(0)
     turn(order[0])
     m1(order[0], 0)
     turn(order[1])
     m1(order[1], 0)
     ends(0, 0)
+    s3[me_t] = reduced(s2, s2_copy, 4)
+    for d in range(1, 8):
+        s3_copy(d).start()
+    ends(1, 0)
     y_pass(1)
+    y_start(2)
+    at_distance(2, z_pass)
+    tok_wait(1)
     turn(order[2])
     m1(order[2], 0)
-    ends(1, 0)
     turn(order[3])
     m1(order[3], 0)
     ends(2, 0)
+    middle(0, 0)
+    y_wait(1, 1)
+    y_wait(1, 2)
+    m1(order[0], 1)
+    m1(order[1], 1)
+    ends(0, 1)
+    middle(1, 0)
+    m1(order[2], 1)
+    ends(1, 1)
+    y_pass(2)
+    m1(order[3], 1)
+    ends(2, 1)
 
     tot = reduced(s3, s3_copy, 8)
     total = jnp.sum(jnp.sum(tot, axis=0, keepdims=True), axis=1, keepdims=True)
@@ -422,17 +440,18 @@
 
     def m3(yy, half):
         yy = yy % 4
-        tt_send[half, yy] = lax.dot_general(
-            ucg[span(yy * TOK, TOK), :], wt[span(half * 512, 512), :],
-            (((1,), (1,)), ((), ())), preferred_element_type=F32,
-        ).astype(BF16)
+        for j in range(2):
+            tt_send[half, yy, :, j * 256:(j + 1) * 256] = lax.dot_general(
+                ucg[span(yy * TOK, TOK), :], wt[span(j * 512 + half * 256, 256), :],
+                (((1,), (1,)), ((), ())), preferred_element_type=F32,
+            ).astype(BF16)
         for d in (2, 1, 3):
             t_send(yy, d, half).start()
 
     def t_send(yy, d, half):
         return rcopy(
-            tt_send.at[half, yy, span(((x + d) % 4) * 64, 64)], tt_recv.at[half, yy, d],
-            tts.at[half, yy, d], ttr.at[half, yy, d], at_x(d),
+            tt_send.at[half, yy, span(((x + d) % 4) * 64, 64)], tt_recv.at[half, yy, d - 1],
+            tts.at[half, yy, d - 1], ttr.at[half, yy, d - 1], at_x(d),
         )
 
     early, late = zl // 2, 1 - zl // 2
@@ -441,39 +460,48 @@
     at_distance(1, tern)
     at_distance(2, tern)
     at_distance(3, z_pass)
+    middle(2, 0)
     m3(y, early)
-    y_wait(1, 1)
+    y_wait(2, 1)
     m3(y + 1, early)
     m3(y + 3, early)
     at_distance(3, tern)
     opposite()
+    middle(0, 1)
+    y_wait(2, 2)
+    m3(y + 2, early)
+    m1(order[0], 2)
+    m1(order[1], 2)
+    ends(0, 2)
+    m2(y + 3, pvf.at[1], pvs.at[1])
+    p_minus(1).start()
+    m2(y + 1, pvs.at[2], pvf.at[1])
+    p_plus(1).start()
+    middle(1, 1)
     m3(y, late)
     m3(y + 1, late)
+    ends(1, 2)
+    m1(order[2], 2)
     m3(y + 3, late)
-    middle(0, 0)
-    y_wait(1, 2)
-    m3(y + 2, early)
     m3(y + 2, late)
-    m1(order[0], 1)
-    m2(y + 3, pvf.at[1], pvs.at[1])
-    p_minus(1).start()
-    ends(0, 1)
-    m2(y + 1, pvs.at[2], pvf.at[1])
-    p_plus(1).start()
-    middle(1, 0)
-    m1(order[1], 1)
-    m1(order[2], 1)
-    ends(1, 1)
-    middle(2, 0)
+    ends(2, 2)
+    middle(2, 1)
+    m1(order[3], 2)
 
     def z_copy(half):
-        return rcopy(zsend.at[half], zrecv.at[half], zxs.at[half], zxr.at[half], flip)
-
-    def f_send(yy, half):
-        return rcopy(fsend.at[half, yy], tgr.at[span(x * 64, 64)], fs.at[half, yy], fr.at[x], final_dev(yy, half))
-
-    def f_recv(xx):
-        return rcopy(fsend.at[0, 0], tgr.at[span(xx * 64, 64)], fs.at[0, 0], fr.at[xx], final_dev(0, 0))
+        return rcopy(tgr.at[half, 1 - zh], zrecv.at[half], zxs.at[half], zxr.at[half], flip)
+
+    def f_send(yy, j, half):
+        return rcopy(
+            fsend.at[half, yy, j], tgr.at[half, y // 2, span(x * 64, 64)],
+            fs.at[half, yy, j], fr.at[half, y // 2, x], final_dev(yy, j),
+        )
+
+    def f_recv(z, xx, half):
+        return rcopy(
+            fsend.at[half, 0, 0], tgr.at[half, z, span(xx * 64, 64)],
+            fs.at[half, 0, 0], fr.at[half, z, xx], final_dev(0, 0),
+        )
 
     def sum_x(half):
         for i in (0, 1, 3, 2):
@@ -486,28 +514,27 @@
                 rows = span(r * 16, 16)
                 total = tt_send[half, yy, span(x * 64 + r * 16, 16), :].astype(F32)
                 for d in range(1, 4):
-                    total = total + tt_recv[half, yy, d, rows, :].astype(F32)
-                tt_own[half, yy, rows, :] = total
-                zsend[half, yy, rows, :] = total.astype(BF16)
-
-        @pl.when(jnp.logical_not(collects))
-        def _():
-            z_copy(half).start()
-
-    def sum_z(half):
-        @pl.when(collects)
-        def _():
-            z_copy(half).wait_recv()
-            for yy in range(4):
-                fsend[half, yy] = (tt_own[half, yy] + zrecv[half, yy].astype(F32)).astype(BF16)
-
-                @pl.when(jnp.logical_not(final_self(yy, half)))
+                    total = total + tt_recv[half, yy, d - 1, rows, :].astype(F32)
+                fsend[half, yy, 0, rows, :] = total[:, 0:256].astype(BF16)
+                fsend[half, yy, 1, rows, :] = total[:, 256:512].astype(BF16)
+
+            for j in range(2):
+                @pl.when(jnp.logical_not(final_self(yy, j)))
                 def _():
-                    f_send(yy, half).start()
-
-                @pl.when(final_self(yy, half))
+                    f_send(yy, j, half).start()
+
+                @pl.when(final_self(yy, j))
                 def _():
-                    tgr[span(x * 64, 64), :] = fsend[half, yy]
+                    tgr[half, y // 2, span(x * 64, 64), :] = fsend[half, yy, j]
+
+    def to_z(half):
+        for z in range(2):
+            for xx in range(4):
+                @pl.when(jnp.logical_not(source_self(z, xx)))
+                def _():
+                    f_recv(z, xx, half).wait_recv()
+
+        z_copy(half).start()
 
     def add_fwd(slot, h):
         @pl.loop(h * 8, h * 8 + 8)
@@ -516,21 +543,49 @@
             pvs[slot, rows, :] = (pvf[1, rows, :] + fwd[rows, :].astype(F32)).astype(BF16)
 
     sum_x(early)
-    ends(2, 1)
-    m1(order[3], 1)
+    middle(0, 2)
+    m2(y, pvf.at[0], pvf.at[0])
+    middle(1, 2)
     p_minus(0).wait_recv()
     add_fwd(1, 0)
-    p_minus(2).start()
     p_plus(0).wait_recv()
     add_fwd(2, 1)
+    middle(2, 2)
+    sum_x(late)
+    p_minus(2).start()
     p_plus(2).start()
-    middle(0, 1)
-    sum_x(late)
-    m2(y, pvf.at[0], pvf.at[0])
-    middle(1, 1)
-    sum_z(early)
-    middle(2, 1)
-    sum_z(late)
+    to_z(early)
+
+    for d in range(1, 4):
+        tok_send(d).wait_send()
+        s2_copy(d).wait_send()
+        for b in range(4):
+            t_send(b, d, 0).wait_send()
+            t_send(b, d, 1).wait_send()
+        for e in range(1, 4):
+            tok_share(d, e, 0).wait_send()
+            tok_share(d, e, 1).wait_send()
+    for d in range(1, 8):
+        s1_copy(d).wait_send()
+        s3_copy(d).wait_send()
+    for i in range(3):
+        for h in range(3):
+            y_right(h, i).wait_send()
+            y_left(h, i).wait_send()
+    for b in range(4):
+        c_send(b).wait_send()
+        for h in range(3):
+            g_cross(b, h).wait_send()
+
+        @pl.when(jnp.logical_and(zl < 3, b <= zl))
+        def _():
+            z_right(b).wait_send()
+
+        @pl.when(jnp.logical_and(zl > 0, b >= zl))
+        def _():
+            z_left(b).wait_send()
+
+    to_z(late)
 
     def finish(h):
         @pl.loop(h * 8, h * 8 + 8)
@@ -547,7 +602,7 @@
     p_plus(2).wait_recv()
     finish(1)
 
-    for h in range(2):
+    for h in range(3):
         g_cross(zl, h).wait_recv()
         up_out[:, cols(h)] = gp[zl, :, cols(h)] + gxr[zl, :, cols(h)].astype(F32)
 
@@ -561,62 +616,32 @@
             g_left(zl, h).wait_recv()
             up_out[:, cols(h)] += grr[zl, :, cols(h)].astype(F32)
 
-    for xx in range(4):
-        @pl.when(jnp.logical_not(source_self(xx)))
-        def _():
-            f_recv(xx).wait_recv()
-
-    token_out[...] = tgr[...]
-
-    for d in range(1, 4):
-        tok_send(d).wait_send()
-        s2_copy(d).wait_send()
-        for b in range(4):
-            t_send(b, d, 0).wait_send()
-            t_send(b, d, 1).wait_send()
-        for e in range(1, 4):
-            tok_share(d, e).wait_send()
-    for d in range(1, 8):
-        s1_copy(d).wait_send()
-        s3_copy(d).wait_send()
+    for half in (early, late):
+        z_copy(half).wait_recv()
+        token_out[:, span(half * 256, 256)] = (
+            tgr[half, zh].astype(F32) + zrecv[half].astype(F32)
+        ).astype(BF16)
+
     for i in range(3):
-        for h in range(2):
-            y_right(h, i).wait_send()
-            y_left(h, i).wait_send()
         p_minus(i).wait_send()
         p_plus(i).wait_send()
     for b in range(4):
-        c_send(b).wait_send()
-        g_cross(b, 0).wait_send()
-        g_cross(b, 1).wait_send()
-
-        @pl.when(jnp.logical_and(zl < 3, b <= zl))
-        def _():
-            z_right(b).wait_send()
-
-        @pl.when(jnp.logical_and(zl > 0, b >= zl))
-        def _():
-            z_left(b).wait_send()
-
-        @pl.when(b > zl)
-        def _():
-            g_right(b, 0).wait_send()
-            g_right(b, 1).wait_send()
-
-        @pl.when(b < zl)
-        def _():
-            g_left(b, 0).wait_send()
-            g_left(b, 1).wait_send()
+        for h in range(3):
+            @pl.when(b > zl)
+            def _():
+                g_right(b, h).wait_send()
+
+            @pl.when(b < zl)
+            def _():
+                g_left(b, h).wait_send()
 
     for half in range(2):
-        @pl.when(jnp.logical_not(collects))
-        def _():
-            z_copy(half).wait_send()
-
+        z_copy(half).wait_send()
         for yy in range(4):
-            @pl.when(jnp.logical_and(collects, jnp.logical_not(final_self(yy, half))))
-            def _():
-                f_send(yy, half).wait_send()
+            for j in range(2):
+                @pl.when(jnp.logical_not(final_self(yy, j)))
+                def _():
+                    f_send(yy, j, half).wait_send()
 
 
 def on_device(tokens, gate_values, up_latent, hidden_grad):
@@ -655,21 +680,19 @@
             vm((TOK, COLS), BF16),
             vm((TOK, COLS), BF16),
             vm((2, 4, TOK, 512), BF16),
-            vm((2, 4, 4, 64, 512), BF16),
-            vm((2, 4, 64, 512), F32),
-            vm((2, 4, 64, 512), BF16),
-            vm((2, 4, 64, 512), BF16),
-            vm((2, 4, 64, 512), BF16),
-            vm((TOK, 512), BF16),
+            vm((2, 4, 3, 64, 512), BF16),
+            vm((2, TOK, 256), BF16),
+            vm((2, 4, 2, 64, 256), BF16),
+            vm((2, 2, TOK, 256), BF16),
             vm((8, 8, 128), F32),
             vm((4, 8, 128), F32),
             vm((8, 8, 128), F32),
             dma((4,)),
             dma((4,)), dma((4,)), dma((4,)), dma((4,)), dma((4,)),
-            dma((2, 3)), dma((2, 3)), dma((2, 3)), dma((2, 3)), dma((4,)), dma((4,)), dma((4, 4)), dma((4, 4)),
+            dma((3, 3)), dma((3, 3)), dma((3, 3)), dma((3, 3)), dma((4,)), dma((4,)), dma((3, 3, 2)), dma((3, 3, 2)),
             dma((8,)), dma((8,)), dma((4,)), dma((4,)), dma((8,)), dma((8,)),
-            dma((4, 2)), dma((4, 2)), dma((4, 2)), dma((4, 2)), dma((4, 2)), dma((4, 2)),
-            dma((2, 3)), dma((2, 3)), dma((2, 4, 4)), dma((2, 4, 4)), dma((2,)), dma((2,)), dma((2, 4)), dma((4,)),
+            dma((4, 3)), dma((4, 3)), dma((4, 3)), dma((4, 3)), dma((4, 3)), dma((4, 3)),
+            dma((2, 3)), dma((2, 3)), dma((2, 4, 3)), dma((2, 4, 3)), dma((2,)), dma((2,)), dma((2, 4, 2)), dma((2, 2, 4)),
         ],
         compiler_params=pltpu.CompilerParams(
             collective_id=0, has_side_effects=True, vmem_limit_bytes=60 * 1024 * 1024

time: 103 us -> 99 us (0.961)
  the two profiles are of different devices: /device:TPU:19 before, /device:TPU:8 now
where the time goes in v4:
time: 99 us; the launch traced here: 98 us
  Pallas kernels  93.8 us (95%)
  local copies, waits for them, and re-layouts  3.47 us (4%)
    pallas_call x1, Pallas kernels, on_device(): pl.pallas_call(kernel, out_shape=(vm((TOK, COLS), BF16), vm((TOK, COLS),...  93.8 us
    unnamed x4, local copies, waits for them, and re-layouts  3.47 us

profile of v4, /device:TPU:8, one launch (start us, length us, event | category | flops | bytes accessed | tf_op | source)
XLA Modules:
  0.0 98.0 jit_solution(11158922222969301990)
XLA Ops:
  0.6 93.8 %shard_map.75 = (bf16[256,1792]{1,0:T(8,128)(2,1)S(1)}, bf16[256,1792]{1,0:T(8,128)(2,1)S(1)}, bf16[256,512]{1,0:T(8,128)(2,1)S(1)}, f32[128,1792]{1,0:T(8,128)S(1)}) custom-call(bf16[256,4096]{1,0:T(8,128)(2,1)} %tokens.1, bf16[256,1792]{1,0:T(8,128)(2,1)} %gate.1, f32[128,1792]{1,0:T(8,128)} %latent.1, bf16[256,1792]{1,0:T(8,128)(2,1)} %cot.1), custom_call_target="tpu_custom_call" | custom-call | tf_op jit(solution)/shard_map/pallas_call | solution.py:650
  94.5 0.9 copy.12
  95.4 0.7 copy.14
  96.1 0.9 copy.13
  97.0 0.9 copy.15

commit v5 on v4

--- a/solution.py
+++ b/solution.py
@@ -31,7 +31,7 @@
     in_sem, zr_sem, zsr_sem, zsl_sem, cs_sem, cr_sem,
     yrs, yrr, yls, ylr, tks, tkr, txs, txr,
     s1s, s1r, s2s, s2r, s3s, s3r,
-    gcs, gcr, gls, glr, grs, grr_sem,
+    gcs, gcr, glr, grs, grr_sem,
     ops, opr, tts, ttr, zxs, zxr, fs, fr,
 ):
     me_dp = lax.axis_index("dp")
@@ -97,7 +97,10 @@
         greet(at_y(d))
     for d in range(1, 8):
         greet((y * 8 + (g8 + d) % 8, me_t))
-        greet((me_dp, (me_t + d) % 8))
+    for d in range(1, 4):
+        greet(at_x(d))
+    for d in range(8):
+        greet((y * 8 + d, (1 - zh) * 4 + x))
 
     for z in range(2):
         for xx in range(4):
@@ -109,7 +112,7 @@
     for yy in range(4):
         for j in range(2):
             takers = takers - jnp.where(final_self(yy, j), 1, 0)
-    pl.semaphore_wait(barrier, 17 + takers)
+    pl.semaphore_wait(barrier, 21 + takers)
 
     def tok_send(d):
         yy = (y + d) % 4
@@ -122,7 +125,7 @@
     def tok_share(d, e, c):
         half = zl // 2 if c else 1 - zl // 2
         piece = tokg.at[span(((y + 4 - d) % 4) * TOK + x * 64, 64), span(half * 512, 512)]
-        return rcopy(piece, piece, txs.at[d - 1, e - 1, c], txr.at[d - 1, e - 1, c], at_x(e))
+        return rcopy(piece, piece, txs.at[c], txr.at[c], at_x(e))
 
     for d in (1, 3, 2):
         tok_send(d).start()
@@ -154,18 +157,20 @@
     def c_recv(b):
         return rcopy(wg.at[b, k], wg.at[b, 1 - k], cs_sem.at[b], cr_sem.at[b], other)
 
-    s1[g8] = part
+    me16 = zh * 8 + g8
+    s1[me16] = part
 
     def s1_copy(d):
-        return rcopy(s1.at[g8], s1.at[g8], s1s.at[d], s1r.at[d], (y * 8 + (g8 + d) % 8, me_t))
+        to = (me16 + d) % 16
+        return rcopy(s1.at[me16], s1.at[me16], s1s, s1r, (y * 8 + to % 8, (to // 8) * 4 + x))
 
     def s2_copy(d):
-        return rcopy(s2.at[y], s2.at[y], s2s.at[d], s2r.at[d], at_y(d))
+        return rcopy(s2.at[y], s2.at[y], s2s, s2r, at_y(d))
 
     def s3_copy(d):
-        return rcopy(s3.at[me_t], s3.at[me_t], s3s.at[d], s3r.at[d], (me_dp, (me_t + d) % 8))
-
-    for d in range(1, 8):
+        return rcopy(s3.at[x], s3.at[x], s3s, s3r, at_x(d))
+
+    for d in range(1, 16):
         s1_copy(d).start()
 
     @pl.when(zl < 3)
@@ -198,11 +203,11 @@
 
     def y_right(h, i):
         piece = (uc_part(y, 0, h), uc_part(y, 1, h), uc_part(y + 3, 0, h))[i]
-        return rcopy(piece, piece, yrs.at[h, i], yrr.at[h, i], at_y(1))
+        return rcopy(piece, piece, yrs, yrr.at[h, i], at_y(1))
 
     def y_left(h, i):
         piece = (uc_part(y, 1, h), uc_part(y, 0, h), uc_part(y + 1, 1, h))[i]
-        return rcopy(piece, piece, yls.at[h, i], ylr.at[h, i], at_y(3))
+        return rcopy(piece, piece, yls, ylr.at[h, i], at_y(3))
 
     def y_start(h):
         y_right(h, 0).start()
@@ -223,15 +228,18 @@
     cot_rows(0, 256)
     y_start(0)
 
-    def reduced(slots, copy, n):
-        for d in range(1, n):
-            copy(d).wait_recv()
+    def others(slots, ssem, rsem, n):
+        part = slots.at[pl.ds(0, n - 1)]
+        return rcopy(part, part, ssem, rsem, other)
+
+    def reduced(slots, ssem, rsem, n):
+        others(slots, ssem, rsem, n).wait_recv()
         tot = slots[0]
         for i in range(1, n):
             tot = tot + slots[i]
         return tot
 
-    s2[y] = reduced(s1, s1_copy, 8)
+    s2[y] = reduced(s1, s1s, s1r, 16)
     for d in range(1, 4):
         s2_copy(d).start()
 
@@ -283,10 +291,62 @@
         tokt[target, 0:128, :] = tokg[:, span(target * 256 + k * 128, 128)].T
         tokt[target, 128:256, :] = tokg[:, span(target * 256 + (1 - k) * 128, 128)].T
 
+    def tok_all(c):
+        part = tokg.at[pl.ds(0, 576), pl.ds(0, 512)]
+        return rcopy(part, part, txs.at[c], txr.at[c], at_x(1))
+
     def tok_wait(c):
-        for d in (1, 3, 2):
-            for e in (2, 1, 3):
-                tok_share(d, e, c).wait_recv()
+        tok_all(c).wait_recv()
+
+    def z_copy(half):
+        return rcopy(tgr.at[half, 1 - zh], zrecv.at[half], zxs.at[half], zxr.at[half], flip)
+
+    def f_send(yy, j, half):
+        return rcopy(
+            fsend.at[half, yy, j], tgr.at[half, y // 2, span(x * 64, 64)],
+            fs.at[half, yy, j], fr.at[half, y // 2, x], final_dev(yy, j),
+        )
+
+    def f_recv(z, xx, half):
+        return rcopy(
+            fsend.at[half, 0, 0], tgr.at[half, z, span(xx * 64, 64)],
+            fs.at[half, 0, 0], fr.at[half, z, xx], final_dev(0, 0),
+        )
+
+    def t_all(half):
+        return rcopy(tt_recv.at[half], tt_recv.at[half], tts.at[half], ttr.at[half], at_x(1))
+
+    def sum_x(half):
+        t_all(half).wait_recv()
+        for i in (0, 1, 3, 2):
+            yy = (y + i) % 4
+
+            @pl.loop(0, 4)
+            def _(r):
+                rows = span(r * 16, 16)
+                total = tt_send[half, yy, span(x * 64 + r * 16, 16), :].astype(F32)
+                for d in range(1, 4):
+                    total = total + tt_recv[half, yy, d - 1, rows, :].astype(F32)
+                fsend[half, yy, 0, rows, :] = total[:, 0:256].astype(BF16)
+                fsend[half, yy, 1, rows, :] = total[:, 256:512].astype(BF16)
+
+            for j in range(2):
+                @pl.when(jnp.logical_not(final_self(yy, j)))
+                def _():
+                    f_send(yy, j, half).start()
+
+                @pl.when(final_self(yy, j))
+                def _():
+                    tgr[half, y // 2, span(x * 64, 64), :] = fsend[half, yy, j]
+
+    def to_z(half):
+        for z in range(2):
+            for xx in range(4):
+                @pl.when(jnp.logical_not(source_self(z, xx)))
+                def _():
+                    f_recv(z, xx, half).wait_recv()
+
+        z_copy(half).start()
 
     def m1(target, h):
         term = jnp.dot(tokt[target], ucg[:, cols(h)], preferred_element_type=F32)
@@ -298,7 +358,7 @@
         return ref.at[target, :, cols(h)]
 
     def g_cross(target, h):
-        return rcopy(part_of(gxs, target, h), part_of(gxr, target, h), gcs.at[target, h], gcr.at[target, h], other)
+        return rcopy(part_of(gxs, target, h), part_of(gxr, target, h), gcs, gcr.at[target, h], other)
 
     def g_right(target, h):
         return rcopy(
@@ -309,7 +369,7 @@
     def g_left(target, h):
         return rcopy(
             part_of(gsend, target, h), part_of(grr, target, h),
-            gls.at[target, h], grr_sem.at[target, h], at_z(lax.rem(zl + 3, 4)),
+            grs.at[target, h], grr_sem.at[target, h], at_z(lax.rem(zl + 3, 4)),
         )
 
     def add_up(target, h, extra):
@@ -397,8 +457,8 @@
     turn(order[1])
     m1(order[1], 0)
     ends(0, 0)
-    s3[me_t] = reduced(s2, s2_copy, 4)
-    for d in range(1, 8):
+    s3[x] = reduced(s2, s2s, s2r, 4)
+    for d in range(1, 4):
         s3_copy(d).start()
     ends(1, 0)
     y_pass(1)
@@ -411,19 +471,7 @@
     m1(order[3], 0)
     ends(2, 0)
     middle(0, 0)
-    y_wait(1, 1)
-    y_wait(1, 2)
-    m1(order[0], 1)
-    m1(order[1], 1)
-    ends(0, 1)
-    middle(1, 0)
-    m1(order[2], 1)
-    ends(1, 1)
-    y_pass(2)
-    m1(order[3], 1)
-    ends(2, 1)
-
-    tot = reduced(s3, s3_copy, 8)
+    tot = reduced(s3, s3s, s3r, 4)
     total = jnp.sum(jnp.sum(tot, axis=0, keepdims=True), axis=1, keepdims=True)
     scale = total / (D * FF) + EPSILON
     bound = 0.5 * scale
@@ -451,17 +499,29 @@
     def t_send(yy, d, half):
         return rcopy(
             tt_send.at[half, yy, span(((x + d) % 4) * 64, 64)], tt_recv.at[half, yy, d - 1],
-            tts.at[half, yy, d - 1], ttr.at[half, yy, d - 1], at_x(d),
+            tts.at[half], ttr.at[half], at_x(d),
         )
 
     early, late = zl // 2, 1 - zl // 2
 
     tern(zl)
     at_distance(1, tern)
+    y_wait(1, 1)
+    y_wait(1, 2)
+    m1(order[0], 1)
+    m1(order[1], 1)
+    ends(0, 1)
+    middle(1, 0)
+    m1(order[2], 1)
+    ends(1, 1)
     at_distance(2, tern)
+    m3(y, early)
+    y_pass(2)
+    m1(order[3], 1)
+    ends(2, 1)
+
     at_distance(3, z_pass)
     middle(2, 0)
-    m3(y, early)
     y_wait(2, 1)
     m3(y + 1, early)
     m3(y + 3, early)
@@ -473,68 +533,21 @@
     m1(order[0], 2)
     m1(order[1], 2)
     ends(0, 2)
-    m2(y + 3, pvf.at[1], pvs.at[1])
-    p_minus(1).start()
-    m2(y + 1, pvs.at[2], pvf.at[1])
-    p_plus(1).start()
-    middle(1, 1)
     m3(y, late)
     m3(y + 1, late)
-    ends(1, 2)
-    m1(order[2], 2)
     m3(y + 3, late)
     m3(y + 2, late)
+    m2(y + 3, pvf.at[1], pvs.at[1])
+    m2(y + 1, pvs.at[2], pvf.at[1])
+    sum_x(early)
+    p_minus(1).start()
+    p_plus(1).start()
+    ends(1, 2)
+    middle(1, 1)
+    m1(order[2], 2)
     ends(2, 2)
     middle(2, 1)
     m1(order[3], 2)
-
-    def z_copy(half):
-        return rcopy(tgr.at[half, 1 - zh], zrecv.at[half], zxs.at[half], zxr.at[half], flip)
-
-    def f_send(yy, j, half):
-        return rcopy(
-            fsend.at[half, yy, j], tgr.at[half, y // 2, span(x * 64, 64)],
-            fs.at[half, yy, j], fr.at[half, y // 2, x], final_dev(yy, j),
-        )
-
-    def f_recv(z, xx, half):
-        return rcopy(
-            fsend.at[half, 0, 0], tgr.at[half, z, span(xx * 64, 64)],
-            fs.at[half, 0, 0], fr.at[half, z, xx], final_dev(0, 0),
-        )
-
-    def sum_x(half):
-        for i in (0, 1, 3, 2):
-            yy = (y + i) % 4
-            for d in range(1, 4):
-                t_send(yy, d, half).wait_recv()
-
-            @pl.loop(0, 4)
-            def _(r):
-                rows = span(r * 16, 16)
-                total = tt_send[half, yy, span(x * 64 + r * 16, 16), :].astype(F32)
-                for d in range(1, 4):
-                    total = total + tt_recv[half, yy, d - 1, rows, :].astype(F32)
-                fsend[half, yy, 0, rows, :] = total[:, 0:256].astype(BF16)
-                fsend[half, yy, 1, rows, :] = total[:, 256:512].astype(BF16)
-
-            for j in range(2):
-                @pl.when(jnp.logical_not(final_self(yy, j)))
-                def _():
-                    f_send(yy, j, half).start()
-
-                @pl.when(final_self(yy, j))
-                def _():
-                    tgr[half, y // 2, span(x * 64, 64), :] = fsend[half, yy, j]
-
-    def to_z(half):
-        for z in range(2):
-            for xx in range(4):
-                @pl.when(jnp.logical_not(source_self(z, xx)))
-                def _():
-                    f_recv(z, xx, half).wait_recv()
-
-        z_copy(half).start()
 
     def add_fwd(slot, h):
         @pl.loop(h * 8, h * 8 + 8)
@@ -542,7 +555,6 @@
             rows = span(i * 16, 16)
             pvs[slot, rows, :] = (pvf[1, rows, :] + fwd[rows, :].astype(F32)).astype(BF16)
 
-    sum_x(early)
     middle(0, 2)
     m2(y, pvf.at[0], pvf.at[0])
     middle(1, 2)
@@ -551,32 +563,26 @@
     p_plus(0).wait_recv()
     add_fwd(2, 1)
     middle(2, 2)
+    to_z(early)
     sum_x(late)
     p_minus(2).start()
     p_plus(2).start()
-    to_z(early)
-
+
+    t_all(0).wait_send()
+    t_all(1).wait_send()
+    tok_all(0).wait_send()
+    tok_all(1).wait_send()
     for d in range(1, 4):
         tok_send(d).wait_send()
-        s2_copy(d).wait_send()
-        for b in range(4):
-            t_send(b, d, 0).wait_send()
-            t_send(b, d, 1).wait_send()
-        for e in range(1, 4):
-            tok_share(d, e, 0).wait_send()
-            tok_share(d, e, 1).wait_send()
-    for d in range(1, 8):
-        s1_copy(d).wait_send()
-        s3_copy(d).wait_send()
-    for i in range(3):
-        for h in range(3):
-            y_right(h, i).wait_send()
-            y_left(h, i).wait_send()
+    others(s1, s1s, s1r, 16).wait_send()
+    others(s2, s2s, s2r, 4).wait_send()
+    others(s3, s3s, s3r, 4).wait_send()
+    rcopy(gxs, gxr, gcs, gcr.at[0, 0], other).wait_send()
+    all_sent = ucg.at[pl.ds(0, 384)]
+    rcopy(all_sent, all_sent, yrs, yrr.at[0, 0], at_y(1)).wait_send()
+    rcopy(all_sent, all_sent, yls, ylr.at[0, 0], at_y(3)).wait_send()
     for b in range(4):
         c_send(b).wait_send()
-        for h in range(3):
-            g_cross(b, h).wait_send()
-
         @pl.when(jnp.logical_and(zl < 3, b <= zl))
         def _():
             z_right(b).wait_send()
@@ -684,15 +690,15 @@
             vm((2, TOK, 256), BF16),
             vm((2, 4, 2, 64, 256), BF16),
             vm((2, 2, TOK, 256), BF16),
-            vm((8, 8, 128), F32),
+            vm((16, 8, 128), F32),
             vm((4, 8, 128), F32),
-            vm((8, 8, 128), F32),
+            vm((4, 8, 128), F32),
             dma((4,)),
             dma((4,)), dma((4,)), dma((4,)), dma((4,)), dma((4,)),
-            dma((3, 3)), dma((3, 3)), dma((3, 3)), dma((3, 3)), dma((4,)), dma((4,)), dma((3, 3, 2)), dma((3, 3, 2)),
-            dma((8,)), dma((8,)), dma((4,)), dma((4,)), dma((8,)), dma((8,)),
-            dma((4, 3)), dma((4, 3)), dma((4, 3)), dma((4, 3)), dma((4, 3)), dma((4, 3)),
-            dma((2, 3)), dma((2, 3)), dma((2, 4, 3)), dma((2, 4, 3)), dma((2,)), dma((2,)), dma((2, 4, 2)), dma((2, 2, 4)),
+            dma, dma((3, 3)), dma, dma((3, 3)), dma((4,)), dma((4,)), dma((2,)), dma((2,)),
+            dma, dma, dma, dma, dma, dma,
+            dma, dma((4, 3)), dma((4, 3)), dma((4, 3)), dma((4, 3)),
+            dma((2, 3)), dma((2, 3)), dma((2,)), dma((2,)), dma((2,)), dma((2,)), dma((2, 4, 2)), dma((2, 2, 4)),
         ],
         compiler_params=pltpu.CompilerParams(
             collective_id=0, has_side_effects=True, vmem_limit_bytes=60 * 1024 * 1024

time: 99 us -> 98.3 us (level)
  no operation moved by 1% of the time
where the time goes in v5:
time: 98.3 us; the launch traced here: 98.1 us
  Pallas kernels  94 us (96%)
  local copies, waits for them, and re-layouts  3.47 us (4%)
    pallas_call x1, Pallas kernels, on_device(): pl.pallas_call(kernel, out_shape=(vm((TOK, COLS), BF16), vm((TOK, COLS),...  94 us
    unnamed x4, local copies, waits for them, and re-layouts  3.47 us

profile of v5, /device:TPU:8, one launch (start us, length us, event | category | flops | bytes accessed | tf_op | source)
XLA Modules:
  0.0 98.1 jit_solution(3643660351060924373)
XLA Ops:
  0.6 94.0 %shard_map.75 = (bf16[256,1792]{1,0:T(8,128)(2,1)S(1)}, bf16[256,1792]{1,0:T(8,128)(2,1)S(1)}, bf16[256,512]{1,0:T(8,128)(2,1)S(1)}, f32[128,1792]{1,0:T(8,128)S(1)}) custom-call(bf16[256,4096]{1,0:T(8,128)(2,1)} %tokens.1, bf16[256,1792]{1,0:T(8,128)(2,1)} %gate.1, f32[128,1792]{1,0:T(8,128)} %latent.1, bf16[256,1792]{1,0:T(8,128)(2,1)} %cot.1), custom_call_target="tpu_custom_call" | custom-call | tf_op jit(solution)/shard_map/pallas_call | solution.py:656
  94.6 0.9 copy.12
  95.6 0.7 copy.14
  96.3 0.9 copy.13
  97.2 0.9 copy.15
